TPU v7x, 128 devices: a whole 4x4x4 slice. The times are simulated.
128 devices in a mesh: gx: 16 (over z, y), gy: 8 (over x, core).
Axes of the slice: x: 4, y: 4, z: 4, core: 2. Of those that a mesh axis runs over, the one named last changes fastest.
Arguments:
- latent: bfloat16 [512, 64, 8, 128], P('gx', 'gy'), may hold values from -6 to 6
- position: bfloat16 [512, 64, 3, 8], P('gx', 'gy'), may hold values from 0 to 1
- counts: int32 [512, 64], P('gx', 'gy'), may hold values from 0 to 8, as said below
- leaving: int32 [16, 8, 9, 64], P('gx', 'gy'), may hold values from -1 to 2047, as said below
- landing: int32 [16, 8, 9, 64], P('gx', 'gy'), may hold values from -1 to 2047, as said below
- cotangent: bfloat16 [512, 64, 8, 128], P('gx', 'gy'), may hold values from -6 to 6
- encoder_weight: float32 [4, 128], replicated, may hold values from -1.5 to 1.5
- encoder_bias: float32 [128], replicated, may hold values from -3 to 3
- receiver_weight: bfloat16 [128, 128], replicated, may hold values from -0.3125 to 0.3125
- sender_weight: bfloat16 [128, 128], replicated, may hold values from -0.3125 to 0.3125
- edge_weight: bfloat16 [128, 128], replicated, may hold values from -0.3125 to 0.3125
- edge_bias: float32 [128], replicated, may hold values from -3 to 3
- message_weight: bfloat16 [128, 128], replicated, may hold values from -0.5 to 0.5
- message_bias: float32 [128], replicated, may hold values from -3 to 3
- node_weight: bfloat16 [128, 128], replicated, may hold values from -0.375 to 0.375
- summed_weight: bfloat16 [128, 128], replicated, may hold values from -0.09375 to 0.09375
- node_bias: float32 [128], replicated, may hold values from -3 to 3
- output_weight: bfloat16 [128, 128], replicated, may hold values from -0.5 to 0.5
- output_bias: float32 [128], replicated, may hold values from -3 to 3
- norm_gain: float32 [128], replicated, may hold values from 0.1 to 1.9
Outputs:
- new_latent: bfloat16 [512, 64, 8, 128], P('gx', 'gy')
- latent_grad: float32 [512, 64, 8, 128], P('gx', 'gy')
Inputs may be any that keep to these rules, and one draw needn't show every extreme that they name: `counts`: particles in each cell; some cell holds exactly 8. `leaving`: entry m of direction k of a device names a slot of that device (in the order of the first step) whose particle moves to the device dx = k // 3 - 1, dy = k % 3 - 1 blocks away, periodically; k = 4 keeps it on the device; -1 marks an empty entry; the slots named by one device are distinct; some device fills all 64 entries of some direction. `landing`: entry m of direction k of a device names the slot of that device that receives the particle sent as entry m of direction k by the device dx, dy blocks back; it is -1 exactly where that sender's entry is -1; the slots named by one device are distinct.
All inputs are finite; a program needn't handle non-finite values.
Results may differ from a plain program's by a relative error of at most 0.006.
Values may be sent and summed in bfloat16 or wider, within the bound.
A program may use at most 64 MiB of HBM per device.

v0:
```python
import jax
import jax.numpy as jnp
from jax import lax
from jax.experimental import pallas as pl
from jax.experimental.pallas import tpu as pltpu
from jax.sharding import PartitionSpec as P

ln_eps = 1e-05
F32 = jnp.float32
BF = jnp.bfloat16
BIG_PRE = 4096.0
BIG_H = 131072.0
NH = 18
GROUP = 2


def mm(a, b):
    return jnp.dot(a, b, preferred_element_type=F32)


def mmt(a, b):
    return lax.dot_general(a, b, (((1,), (1,)), ((), ())), preferred_element_type=F32)


def iota(shape, dim):
    return lax.broadcasted_iota(jnp.int32, shape, dim)


def tree(parts):
    parts = list(parts)
    while len(parts) > 1:
        parts = [
            parts[i] + parts[i + 1] if i + 1 < len(parts) else parts[i]
            for i in range(0, len(parts), 2)
        ]
    return parts[0]


def step_of(n):
    return n // 3, n % 3


def edge_kernel(
    wl_ref, geom_ref, cot_ref, ew_ref, eb_ref, rw_ref, sw_ref, dw_ref, db_ref, mw_ref, mb_ref,
    nw_ref, uw_ref, nb_ref, ow_ref, ob_ref, gain_ref,
    upd_ref, grad_ref, send_ref,
    gj_ref, gi_ref, s_ref, r_ref, rel_ref, occ_ref, cnt_ref, w1_ref, bd_ref,
    se_ref, sh_ref, sg_ref, pull_ref, acc_ref, g_ref,
):
    lane = iota((128, 128), 1)
    row = iota((128, 128), 0)
    whole = ew_ref[...]
    high = whole.astype(BF).astype(F32)
    low = whole - high
    bias_high = eb_ref[...].astype(BF).astype(F32)
    bias_low = eb_ref[...] - bias_high
    wide = lambda v: jnp.broadcast_to(v, (8, 128))
    blocks = [wide(high[c : c + 1]) for c in range(3)]
    blocks += [wide(low[c : c + 1]) for c in range(3)]
    blocks += [wide(high[3:4])] * 3 + [wide(low[3:4])] * 3
    blocks += [wide(bias_high), wide(bias_low)]
    blocks += [jnp.ones((16, 128), F32)]
    stacked = jnp.concatenate(blocks, axis=0)
    for p in range(8):
        w1_ref[:, p * 128 : (p + 1) * 128] = jnp.where(row % 8 == p, stacked, 0.0).astype(BF)
    half_w = (dw_ref[...].astype(F32) * 0.5).astype(BF)
    bd_ref[...] = jnp.zeros((256, 256), BF)
    bd_ref[0:128, 0:128] = half_w
    bd_ref[128:256, 128:256] = half_w

    comp = row // 8
    slot = row % 8
    blk = lane // 8
    in_p = lane % 8
    is_pos = blk < 12
    sel_j = jnp.where(
        is_pos & (comp == blk % 3), 1.0, 0.0
    ) + jnp.where((blk == 14) & (comp == 3), BIG_PRE, 0.0)
    sel_j = jnp.where(comp < 4, sel_j, 0.0).astype(BF)
    sel_i = jnp.where(is_pos & (comp == blk % 3) & (slot == in_p), 1.0, 0.0).astype(BF)
    sel_o = jnp.where(comp == 3, 1.0, 0.0).astype(BF)
    const_blk = iota((1, 128), 1) // 8
    const_j = jnp.where((const_blk == 12) | (const_blk == 13), 1.0, 0.0) + jnp.where(
        const_blk == 14, -BIG_PRE, 0.0
    )
    rep80 = jnp.where(iota((80, 16), 0) // 8 == iota((80, 16), 1), 1.0, 0.0).astype(BF)
    own80 = iota((80, 128), 0) % 8 == iota((80, 128), 1) % 8
    near = iota((64, 16), 1) - iota((64, 16), 0) // 8
    band64 = jnp.where((near >= 0) & (near <= 2), 1.0, 0.0).astype(BF)
    sw_half = (sw_ref[...].astype(F32) * 0.5).astype(BF)
    rw_half = (rw_ref[...].astype(F32) * 0.5).astype(BF)
    eb_half = db_ref[...] * 0.5

    def one_row(x):
        slab = wl_ref[pl.ds(pl.multiple_of(x * 80, 16), 80), :]
        geom = geom_ref[x]
        rep = jnp.where(own80, mm(rep80, geom), 0.0).astype(BF)
        gj = mm(rep, sel_j) + const_j
        occ = mm(rep, sel_o)
        s = mm(slab, sw_half) + (occ * BIG_H - BIG_H)
        return slab, geom, gj, occ, s

    @pl.loop(0, NH)
    def _(x):
        parts = [one_row(x), one_row(x + 16)]
        gj_ref[x] = jnp.concatenate([v[2].reshape(10, 8, 128) for v in parts], axis=1)
        s_ref[x] = jnp.concatenate([v[4].reshape(10, 8, 128) for v in parts], axis=1).astype(BF)

    @pl.loop(0, 32)
    def _(x):
        slab, geom, _, occ, _ = one_row(x + 1)
        at = pl.ds(pl.multiple_of(x * 64, 64), 64)
        r_ref[at, :] = mm(slab, rw_half)[8:72] + eb_half
        rel_ref[at, :] = slab.astype(F32)[8:72]
        occ_ref[at, :] = occ[8:72]
        gi_ref[x] = mm(geom, sel_i)
        near_occ = geom_ref[x].astype(F32) + geom.astype(F32) + geom_ref[x + 2].astype(F32)
        cnt_ref[at, :] = mm(mm(band64, near_occ.astype(BF)).astype(BF), sel_o) - 1.0

    lane16 = iota((16, 128), 1)
    row16 = iota((16, 128), 0)
    squared = (lane16 // 8 >= 6) & (lane16 // 8 < 12)
    linear_c = jnp.where(lane16 // 8 < 12, lane16 // 8 % 3, 3)
    eye = jnp.where((lane16 // 8 == 15) & (lane16 % 8 == row16 % 8), -BIG_PRE, 0.0)
    red_row = iota((16 * GROUP, 128 * GROUP), 0)
    red_col = iota((16 * GROUP, 128 * GROUP), 1)
    red = jnp.where(
        (red_row // (8 * GROUP) == red_col // 8 % 2)
        & (red_row // 8 % GROUP == red_col // 128)
        & (red_row % 8 == red_col // 16 % 8),
        1.0,
        0.0,
    ).astype(BF)

    def natural(x, y):
        return (x * 8 + y) * 8

    def forward(i):
        x = i // (8 // GROUP)
        y0 = i % (8 // GROUP) * GROUP
        feats = []
        for c in range(GROUP):
            y = y0 + c
            gi = jnp.concatenate(
                [
                    jnp.broadcast_to(gi_ref[x, pl.ds(y + 1, 1), :], (8, 128)),
                    jnp.broadcast_to(gi_ref[x + 16, pl.ds(y + 1, 1), :], (8, 128)),
                ],
                axis=0,
            )
            for n in range(9):
                dx, dy = step_of(n)
                reach = gj_ref[x + dx, y + dy] - gi
                if dx != 1 or dy != 1:
                    shift = jnp.where(
                        linear_c == 0, F32(dx - 1), jnp.where(linear_c == 1, F32(dy - 1), 0.0)
                    )
                    reach = reach + shift
                value = jnp.where(squared, reach * reach, reach)
                if n == 4:
                    value = value + eye
                feats.append(value.astype(BF))
        feats = jnp.concatenate(feats, axis=0)
        enc_parts = {}
        hid_parts = {}
        slope_parts = {}
        for pp in range(4):
            pre = mm(feats, w1_ref[:, pp * 256 : (pp + 1) * 256])
            enc = jnp.maximum(pre.astype(BF), BF(0))
            hh = mm(enc, bd_ref[...]).astype(BF)
            for half in range(2):
                p = 2 * pp + half
                cols = slice(half * 128, half * 128 + 128)
                own = jnp.where(row16 % 8 == p, -BIG_H, 0.0).astype(BF)
                for c in range(GROUP):
                    y = y0 + c
                    base = natural(x, y) + p
                    r = jnp.concatenate(
                        [
                            jnp.broadcast_to(r_ref[pl.ds(base, 1), :], (8, 128)),
                            jnp.broadcast_to(r_ref[pl.ds(base + 1024, 1), :], (8, 128)),
                        ],
                        axis=0,
                    ).astype(BF)
                    silus, slopes = [], []
                    for n in range(9):
                        dx, dy = step_of(n)
                        at = c * 144 + n * 16
                        h = hh[at : at + 16, cols] + (s_ref[x + dx, y + dy] + r)
                        if n == 4:
                            h = h + own
                        t = jnp.tanh(h)
                        q = BF(1) + t
                        silu = h * q
                        slope = q + silu * (BF(1) - t)
                        g_ref[x * 8 + y, p, n] = slope
                        silus.append(silu)
                        slopes.append(slope)
                    enc_parts[c, p] = tree(
                        [enc[c * 144 + n * 16 : c * 144 + n * 16 + 16, cols] for n in range(9)]
                    )
                    hid_parts[c, p] = tree(silus)
                    slope_parts[c, p] = tree(slopes)
        order = [(c, p) for c in range(GROUP) for p in range(8)]
        for parts, out in ((enc_parts, se_ref), (hid_parts, sh_ref), (slope_parts, sg_ref)):
            total = mm(red, jnp.concatenate([parts[k] for k in order], axis=0))
            base = pl.multiple_of(natural(x, y0), 8 * GROUP)
            out[pl.ds(base, 8 * GROUP), :] = total[: 8 * GROUP]
            out[pl.ds(base + 1024, 8 * GROUP), :] = total[8 * GROUP :]

    @pl.loop(0, 128 // GROUP)
    def _(i):
        forward(i)

    CH = 512

    @pl.loop(0, 2048 // CH)
    def _(k):
        at = pl.ds(pl.multiple_of(k * CH, CH), CH)
        sh = sh_ref[at, :]
        sh_b = sh.astype(BF)
        sh_l = (sh - sh_b.astype(F32)).astype(BF)
        mw = mw_ref[...]
        summed = se_ref[at, :] + mm(sh_b, mw) + mm(sh_l, mw) + cnt_ref[at, :] * mb_ref[...]
        rel = rel_ref[at, :]
        inner = mm(rel.astype(BF), nw_ref[...]) + mm(summed.astype(BF), uw_ref[...]) + nb_ref[...]
        h = inner * 0.5
        t = jnp.tanh(h)
        q = 1.0 + t
        silu = h * q
        dsilu = 0.5 * (q + silu * (1.0 - t))
        output = mm(silu.astype(BF), ow_ref[...]) + ob_ref[...]
        centred = output - jnp.mean(output, axis=-1, keepdims=True)
        inv = lax.rsqrt(jnp.mean(centred * centred, axis=-1, keepdims=True) + ln_eps)
        normed = centred * inv
        occ = occ_ref[at, :]
        gain = gain_ref[...]
        upd_ref[at, :] = (rel + occ * normed * gain).astype(BF)
        cot = cot_ref[at, :].astype(F32)
        gn = occ * cot * gain
        go = (
            (
                gn
                - jnp.mean(gn, axis=-1, keepdims=True)
                - normed * jnp.mean(gn * normed, axis=-1, keepdims=True)
            )
            * inv
        ).astype(BF)
        ginner = (mmt(go, ow_ref[...]) * dsilu).astype(BF)
        gsum = mmt(ginner, uw_ref[...]).astype(BF)
        pull = mmt(gsum, mw) * 0.5
        pull_ref[at, :] = pull
        rgrad = (pull * sg_ref[at, :]).astype(BF)
        grad_ref[at, :] = cot + mmt(ginner, nw_ref[...]) + mmt(rgrad, rw_ref[...])

    acc_ref[...] = jnp.zeros(acc_ref.shape, F32)

    @pl.loop(0, 128)
    def _(i):
        x = i // 8
        y = i % 8
        pulls = []
        for p in range(8):
            base = natural(x, y) + p
            pulls.append(
                jnp.concatenate(
                    [
                        jnp.broadcast_to(pull_ref[pl.ds(base, 1), :], (8, 128)),
                        jnp.broadcast_to(pull_ref[pl.ds(base + 1024, 1), :], (8, 128)),
                    ],
                    axis=0,
                ).astype(BF)
            )
        for n in range(9):
            dx, dy = step_of(n)
            total = tree([g_ref[i, p, n] * pulls[p] for p in range(8)])
            acc_ref[x + dx, y + dy] += total.astype(F32)

    for x in range(34):
        if x < 16:
            send_ref[x] = acc_ref[x, :, 0:8]
        elif x < 18:
            send_ref[x] = acc_ref[x, :, 0:8] + acc_ref[x - 16, :, 8:16]
        else:
            send_ref[x] = acc_ref[x - 16, :, 8:16]


def edge_call(wl, geom, cot, *weights):
    full = pl.BlockSpec(memory_space=pltpu.VMEM)
    return pl.pallas_call(
        edge_kernel,
        out_shape=(
            jax.ShapeDtypeStruct((2048, 128), BF),
            jax.ShapeDtypeStruct((2048, 128), F32),
            jax.ShapeDtypeStruct((34, 10, 8, 128), F32),
        ),
        in_specs=[full] * (3 + len(weights)),
        out_specs=(full, full, full),
        scratch_shapes=[
            pltpu.VMEM((NH, 10, 16, 128), F32),
            pltpu.VMEM((32, 16, 128), F32),
            pltpu.VMEM((NH, 10, 16, 128), BF),
            pltpu.VMEM((2048, 128), F32),
            pltpu.VMEM((2048, 128), F32),
            pltpu.VMEM((2048, 128), F32),
            pltpu.VMEM((2048, 128), F32),
            pltpu.VMEM((128, 1024), BF),
            pltpu.VMEM((256, 256), BF),
            pltpu.VMEM((2048, 128), F32),
            pltpu.VMEM((2048, 128), F32),
            pltpu.VMEM((2048, 128), F32),
            pltpu.VMEM((2048, 128), F32),
            pltpu.VMEM((NH, 10, 16, 128), F32),
            pltpu.VMEM((128, 8, 9, 16, 128), BF),
        ],
        compiler_params=pltpu.CompilerParams(vmem_limit_bytes=62 * 1024 * 1024),
        name="edges",
    )(wl, geom, cot, *weights)


def shifted(array, axis, by):
    size = lax.axis_size(axis)
    return lax.ppermute(array, axis, [(i, (i + by) % size) for i in range(size)])


def extended(array, sides, width):
    for axis, dim in sides:
        size, length = (lax.axis_size(axis), array.shape[dim])
        up = [(i, (i + 1) % size) for i in range(size)]
        down = [(j, i) for i, j in up]
        last = lax.slice_in_dim(array, length - width, length, axis=dim)
        first = lax.slice_in_dim(array, 0, width, axis=dim)
        before = lax.ppermute(last, axis, up)
        after = lax.ppermute(first, axis, down)
        array = jnp.concatenate([before, array, after], axis=dim)
    return array


def on_device(
    latent, position, counts, leaving, landing, cotangent, encoder_weight, encoder_bias,
    receiver_weight, sender_weight, edge_weight, edge_bias, message_weight, message_bias,
    node_weight, summed_weight, node_bias, output_weight, output_bias, norm_gain,
):
    rows_x, width_y, slot_count, latent_width = latent.shape
    slot_total = rows_x * width_y * slot_count
    capacity = leaving.shape[3]
    flat_rows = latent.reshape(slot_total, latent_width)
    depart = leaving.reshape(9, capacity)
    arrive = landing.reshape(9, capacity)
    picked = flat_rows[jnp.clip(depart, 0, slot_total - 1)]
    picked = jnp.where((depart >= 0)[..., None], picked, jnp.zeros_like(picked))
    grouped = picked.reshape(3, 3, capacity, latent_width)
    along_x = [None, grouped[1], None]
    for step_by in (1, -1):
        along_x[step_by + 1] = shifted(grouped[step_by + 1], "gx", step_by)
    half_moved = jnp.stack(along_x, axis=0)
    along_y = [None, half_moved[:, 1], None]
    for step_by in (1, -1):
        along_y[step_by + 1] = shifted(half_moved[:, step_by + 1], "gy", step_by)
    arrived = jnp.stack(along_y, axis=1).reshape(9, capacity, latent_width)
    target_slots = jnp.where(arrive >= 0, arrive, slot_total).reshape(-1)
    relocated = flat_rows.at[target_slots].set(arrived.reshape(-1, latent_width), mode="drop")
    relocated = relocated.reshape(rows_x, width_y, slot_count, latent_width)
    occupied = (jnp.arange(slot_count)[None, None, :] < counts[:, :, None]).astype(BF)
    geometry = jnp.concatenate([position, occupied[:, :, None, :]], axis=2)
    wide_latent = extended(relocated, (("gx", 0), ("gy", 1)), 1)
    wide_geometry = extended(geometry, (("gx", 0), ("gy", 1)), 1)
    wide_geometry = jnp.pad(wide_geometry.reshape(34, 10, 32), ((0, 0), (0, 6), (0, 96)))
    line = lambda v: v.reshape(1, -1)
    updated, grad, folded = edge_call(
        wide_latent.reshape(-1, latent_width), wide_geometry,
        cotangent.reshape(slot_total, latent_width), encoder_weight, line(encoder_bias),
        receiver_weight, sender_weight, edge_weight, line(edge_bias), message_weight,
        line(message_bias), node_weight, summed_weight, line(node_bias), output_weight,
        line(output_bias), line(norm_gain),
    )
    for step_by in (1, -1):
        edge_row = folded[rows_x + 1] if step_by == 1 else folded[0]
        incoming = shifted(edge_row.astype(jnp.bfloat16), "gx", step_by).astype(edge_row.dtype)
        if step_by == 1:
            folded = folded.at[1].add(incoming)
        else:
            folded = folded.at[rows_x].add(incoming)
    middle_rows = folded[1 : rows_x + 1]
    for step_by in (1, -1):
        column = middle_rows[:, width_y + 1] if step_by == 1 else middle_rows[:, 0]
        incoming = shifted(column.astype(jnp.bfloat16), "gy", step_by).astype(column.dtype)
        if step_by == 1:
            middle_rows = middle_rows.at[:, 1].add(incoming)
        else:
            middle_rows = middle_rows.at[:, width_y].add(incoming)
    send_core = middle_rows[:, 1 : width_y + 1]
    grad = grad + lax.dot_general(
        send_core.astype(BF).reshape(slot_total, latent_width), sender_weight,
        (((1,), (1,)), ((), ())), preferred_element_type=F32,
    )
    return updated.reshape(latent.shape), grad.reshape(latent.shape)


def solution(mesh):
    split = P("gx", "gy", None, None)
    return jax.shard_map(
        on_device,
        mesh=mesh,
        in_specs=(split, split, P("gx", "gy"), split, split, split) + (P(),) * 14,
        out_specs=(split, split),
        check_vma=False,
    )
```

profile of v0, /device:TPU:0, one launch (start us, length us, event | category | flops | bytes accessed | tf_op | source)
XLA Modules:
  0.0 153.4 jit_solution(10224273467341319160)
XLA Ops:
  0.6 0.0 copy-start.1
  0.6 0.0 copy-start.4
  0.7 1.1 copy.52
  1.7 0.7 broadcast_compare_fusion
  2.4 0.7 fusion.11
  3.1 0.1 reshape.299
  3.2 1.9 %gather_fusion = bf16[576,128]{1,0:T(8,128)(2,1)S(1)} fusion(bf16[2048,128]{1,0:T(8,128)(2,1)S(1)} %bitcast.75, s32[1024]{0:T(1024)S(1)} %pad_clamp_fusion), kind=kCustom, calls=%fused_computation | custom fusion | bytes 297216 | tf_op jit(solution)/shard_map/gather | solution.py:350
  5.2 0.1 broadcast_select_fusion
  5.3 6.6 %collective-permute-start = (bf16[3,64,128]{2,1,0:T(8,128)(2,1)S(1)}, bf16[3,64,128]{2,1,0:T(8,128)(2,1)S(1)}, u32[]{:S(2)}, u32[]{:S(2)}) collective-permute-start(bf16[3,64,128]{2,1,0:T(8,128)(2,1)S(1)} %get-tuple-element.65), channel_id=1, source_target_pairs={{0,120},{8,0},{16,8},{24,16},{32,24},{40,32},{48,40},{56,48},{64,5... | collective-permute-start | bytes 147464 | tf_op jit(solution)/shard_map/ppermute | solution.py:323
  12.0 0.0 collective-permute-start.1
  12.0 0.0 copy-done.1
  12.0 0.1 slice_maximum_fusion
  12.1 0.1 collective-permute-start.8
  12.2 5.4 %collective-permute-start.9 = (bf16[1,8,4,8]{0,3,2,1:T(8,128)(2,1)S(1)}, bf16[1,8,4,8]{0,3,2,1:T(8,128)(2,1)S(1)}, u32[]{:S(2)}, u32[]{:S(2)}) collective-permute-start(bf16[1,8,4,8]{0,3,2,1:T(8,128)(2,1)S(1)} %get-tuple-element.69), channel_id=1, source_target_pairs={{8,0},{16,8},{24,16},{32,24},{40,32},{48,40},{56,48},{64,56},{72,6... | collective-permute-start | bytes 1544 | tf_op jit(solution)/shard_map/ppermute | solution.py:334
  17.6 0.0 copy-done.3
  17.6 0.1 reshape.275
  17.7 0.0 collective-permute-done
  17.7 1.7 %collective-permute-done.1 = bf16[3,64,128]{2,1,0:T(8,128)(2,1)S(1)} collective-permute-done((bf16[3,64,128]{2,1,0:T(8,128)(2,1)S(1)}, bf16[3,64,128]{2,1,0:T(8,128)(2,1)S(1)}, u32[]{:S(2)}, u32[]{:S(2)}) %collective-permute-start.1) | collective-permute-done | bytes 49184 | tf_op jit(solution)/shard_map/ppermute | solution.py:323
  19.4 0.8 collective-permute-start.2
  20.2 0.0 collective-permute-start.3
  20.2 1.7 %collective-permute-done.2 = bf16[3,64,128]{2,1,0:T(8,128)(2,1)S(1)} collective-permute-done((bf16[3,64,128]{2,1,0:T(8,128)(2,1)S(1)}, bf16[3,64,128]{2,1,0:T(8,128)(2,1)S(1)}, u32[]{:S(2)}, u32[]{:S(2)}) %collective-permute-start.2) | collective-permute-done | bytes 49184 | tf_op jit(solution)/shard_map/ppermute | solution.py:323
  22.0 3.0 %collective-permute-done.3 = bf16[3,64,128]{2,1,0:T(8,128)(2,1)S(1)} collective-permute-done((bf16[3,64,128]{2,1,0:T(8,128)(2,1)S(1)}, bf16[3,64,128]{2,1,0:T(8,128)(2,1)S(1)}, u32[]{:S(2)}, u32[]{:S(2)}) %collective-permute-start.3) | collective-permute-done | bytes 49184 | tf_op jit(solution)/shard_map/ppermute | solution.py:323
  25.0 4.5 %scatter_fusion = bf16[2048,128]{1,0:T(8,128)(2,1)S(1)} fusion(bf16[2048,128]{1,0:T(8,128)(2,1)S(1)} %bitcast.76, s32[576]{0:T(1024)S(1)} %fusion.12, bf16[576,128]{1,0:T(8,128)(2,1)S(1)} %bitcast.82), kind=kCustom, calls=%fused_computation.1 | custom fusion | bytes 444672 | tf_op jit(solution)/shard_map/scatter | solution.py:362
  29.5 0.1 collective-permute-start.4
  29.6 5.3 %collective-permute-start.5 = (bf16[1,8,8,128]{3,2,1,0:T(8,128)(2,1)S(1)}, bf16[1,8,8,128]{3,2,1,0:T(8,128)(2,1)S(1)}, u32[]{:S(2)}, u32[]{:S(2)}) collective-permute-start(bf16[1,8,8,128]{3,2,1,0:T(8,128)(2,1)S(1)} %get-tuple-element.59), channel_id=1, source_target_pairs={{8,0},{16,8},{24,16},{32,24},{40,32},{48,40},{56,48},{64,56},{72,6... | collective-permute-start | bytes 49160 | tf_op jit(solution)/shard_map/ppermute | solution.py:334
  34.9 0.0 collective-permute-done.8
  35.0 0.0 collective-permute-done.9
  35.0 0.1 pad_maximum_fusion.10
  35.0 0.0 collective-permute-start.10
  35.1 2.9 %collective-permute-start.11 = (bf16[34,1,4,8]{0,3,2,1:T(8,128)(2,1)S(1)}, bf16[34,1,4,8]{0,3,2,1:T(8,128)(2,1)S(1)}, u32[]{:S(2)}, u32[]{:S(2)}) collective-permute-start(bf16[34,1,4,8]{0,3,2,1:T(8,128)(2,1)S(1)} %get-tuple-element.61), channel_id=1, source_target_pairs={{1,0},{2,1},{3,2},{4,3},{5,4},{6,5},{7,6},{0,7},{9,8},{10,9},{11,1... | collective-permute-start | bytes 6536 | tf_op jit(solution)/shard_map/ppermute | solution.py:334
  38.0 0.0 collective-permute-done.4
  38.0 0.0 collective-permute-done.5
  38.1 0.0 collective-permute-start.6
  38.1 2.9 %collective-permute-start.7 = (bf16[34,1,8,128]{3,2,1,0:T(8,128)(2,1)S(1)}, bf16[34,1,8,128]{3,2,1,0:T(8,128)(2,1)S(1)}, u32[]{:S(2)}, u32[]{:S(2)}) collective-permute-start(bf16[34,1,8,128]{3,2,1,0:T(8,128)(2,1)S(1)} %get-tuple-element.57), channel_id=1, source_target_pairs={{1,0},{2,1},{3,2},{4,3},{5,4},{6,5},{7,6},{0,7},{9,8},{10,9},{11,1... | collective-permute-start | bytes 208904 | tf_op jit(solution)/shard_map/ppermute | solution.py:334
  41.0 0.0 collective-permute-done.10
  41.0 0.0 collective-permute-done.11
  41.0 0.1 maximum_bitcast_fusion
  41.1 0.2 copy.32
  41.4 0.7 pad.12.geom_ref
  42.1 0.9 collective-permute-done.6
  43.0 0.0 collective-permute-done.7
  43.0 1.0 pad_maximum_fusion
  44.0 83.1 %edges.1 = (bf16[2048,128]{1,0:T(8,128)(2,1)}, f32[2048,128]{1,0:T(8,128)}, f32[34,10,8,128]{3,2,1,0:T(8,128)}) custom-call(bf16[2720,128]{1,0:T(8,128)(2,1)} %bitcast.79, bf16[34,16,128]{2,1,0:T(8,128)(2,1)} %pad.12.geom_ref, bf16[2048,128]{1,0:T(8,128)(2,1)} %bitcast.84, f32[4,128]{1,0:T(4,128)} %ew_ref.1, f32[1,128]{1,0:T(1,128)} %bitcast.90, ...), custom_call_target="tpu_custom_call" | custom-call | tf_op jit(solution)/shard_map/edges/pallas_call | solution.py:290
  127.2 0.8 fusion.9
  128.0 0.0 collective-permute-start.12
  128.0 7.1 %collective-permute-done.12 = bf16[10,8,128]{2,1,0:T(8,128)(2,1)S(1)} collective-permute-done((bf16[10,8,128]{2,1,0:T(8,128)(2,1)S(1)}, bf16[10,8,128]{2,1,0:T(8,128)(2,1)S(1)}, u32[]{:S(2)}, u32[]{:S(2)}) %collective-permute-start.12) | collective-permute-done | bytes 20512 | tf_op jit(solution)/shard_map/ppermute | solution.py:323
  135.1 1.4 fusion.7
  136.5 0.8 fusion.10
  137.2 0.7 collective-permute-start.13
  137.9 3.1 %collective-permute-done.13 = bf16[10,8,128]{2,1,0:T(8,128)(2,1)S(1)} collective-permute-done((bf16[10,8,128]{2,1,0:T(8,128)(2,1)S(1)}, bf16[10,8,128]{2,1,0:T(8,128)(2,1)S(1)}, u32[]{:S(2)}, u32[]{:S(2)}) %collective-permute-start.13) | collective-permute-done | bytes 20512 | tf_op jit(solution)/shard_map/ppermute | solution.py:323
  141.0 1.4 fusion.6
  142.4 0.9 fusion.4
  143.3 0.0 collective-permute-start.14
  143.3 1.4 slice.228
  144.8 0.0 copy-start.2
  144.8 3.5 %collective-permute-done.14 = bf16[32,8,128]{2,1,0:T(8,128)(2,1)S(1)} collective-permute-done((bf16[32,8,128]{2,1,0:T(8,128)(2,1)S(1)}, bf16[32,8,128]{2,1,0:T(8,128)(2,1)S(1)}, u32[]{:S(2)}, u32[]{:S(2)}) %collective-permute-start.14) | collective-permute-done | bytes 65568 | tf_op jit(solution)/shard_map/ppermute | solution.py:323
  148.2 0.9 fusion.3
  149.2 0.0 collective-permute-start.15
  149.2 1.9 %collective-permute-done.15 = bf16[32,8,128]{2,1,0:T(8,128)(2,1)S(1)} collective-permute-done((bf16[32,8,128]{2,1,0:T(8,128)(2,1)S(1)}, bf16[32,8,128]{2,1,0:T(8,128)(2,1)S(1)}, u32[]{:S(2)}, u32[]{:S(2)}) %collective-permute-start.15) | collective-permute-done | bytes 65568 | tf_op jit(solution)/shard_map/ppermute | solution.py:323
  151.1 0.0 copy-start
  151.1 0.1 slice.266
  151.3 0.3 fusion.14
  151.6 0.8 copy-done
  152.4 1.1 add.61
  (17 shorter events, 0.2 us)
Async XLA Ops:
  0.6 11.4 %copy-start.1 = (bf16[32,8,3,8]{0,3,2,1:T(8,128)(2,1)S(1)}, bf16[32,8,3,8]{0,3,2,1:T(8,128)(2,1)}, u32[]{:S(2)}) copy-start(bf16[32,8,3,8]{0,3,2,1:T(8,128)(2,1)} %param.29) | copy-start | bytes 36868
  0.6 11.3 %copy-start.4 = (s32[32,8]{0,1:T(8,128)S(1)}, s32[32,8]{0,1:T(8,128)}, u32[]{:S(2)}) copy-start(s32[32,8]{0,1:T(8,128)} %param.30) | copy-start | bytes 3076
  0.7 16.9 %copy-start.3 = (s32[1,1,9,64]{3,1,2,0:T(1,128)S(1)}, s32[1,1,9,64]{3,1,2,0:T(1,128)}, u32[]{:S(2)}) copy-start(s32[1,1,9,64]{3,1,2,0:T(1,128)} %param.32) | copy-start | bytes 6916
  5.3 12.4 %collective-permute-start = (bf16[3,64,128]{2,1,0:T(8,128)(2,1)S(1)}, bf16[3,64,128]{2,1,0:T(8,128)(2,1)S(1)}, u32[]{:S(2)}, u32[]{:S(2)}) collective-permute-start(bf16[3,64,128]{2,1,0:T(8,128)(2,1)S(1)} %get-tuple-element.65), channel_id=1, source_target_pairs={{0,120},{8,0},{16,8},{24,16},{32,24},{40,32},{48,40},{56,48},{64,5... | collective-permute-start | bytes 147464 | tf_op jit(solution)/shard_map/ppermute | solution.py:323
  12.0 7.4 %collective-permute-start.1 = (bf16[3,64,128]{2,1,0:T(8,128)(2,1)S(1)}, bf16[3,64,128]{2,1,0:T(8,128)(2,1)S(1)}, u32[]{:S(2)}, u32[]{:S(2)}) collective-permute-start(bf16[3,64,128]{2,1,0:T(8,128)(2,1)S(1)} %get-tuple-element.66), channel_id=1, source_target_pairs={{0,8},{8,16},{16,24},{24,32},{32,40},{40,48},{48,56},{56,64},{64,7... | collective-permute-start | bytes 147464 | tf_op jit(solution)/shard_map/ppermute | solution.py:323
  12.1 22.9 %collective-permute-start.8 = (bf16[1,8,4,8]{0,3,2,1:T(8,128)(2,1)S(1)}, bf16[1,8,4,8]{0,3,2,1:T(8,128)(2,1)S(1)}, u32[]{:S(2)}, u32[]{:S(2)}) collective-permute-start(bf16[1,8,4,8]{0,3,2,1:T(8,128)(2,1)S(1)} %get-tuple-element.68), channel_id=1, source_target_pairs={{0,8},{8,16},{16,24},{24,32},{32,40},{40,48},{48,56},{56,64},{64,7... | collective-permute-start | bytes 1544 | tf_op jit(solution)/shard_map/ppermute | solution.py:333
  12.2 22.8 %collective-permute-start.9 = (bf16[1,8,4,8]{0,3,2,1:T(8,128)(2,1)S(1)}, bf16[1,8,4,8]{0,3,2,1:T(8,128)(2,1)S(1)}, u32[]{:S(2)}, u32[]{:S(2)}) collective-permute-start(bf16[1,8,4,8]{0,3,2,1:T(8,128)(2,1)S(1)} %get-tuple-element.69), channel_id=1, source_target_pairs={{8,0},{16,8},{24,16},{32,24},{40,32},{48,40},{56,48},{64,56},{72,6... | collective-permute-start | bytes 1544 | tf_op jit(solution)/shard_map/ppermute | solution.py:334
  19.4 2.5 %collective-permute-start.2 = (bf16[3,64,128]{2,1,0:T(8,128)(2,1)S(1)}, bf16[3,64,128]{2,1,0:T(8,128)(2,1)S(1)}, u32[]{:S(2)}, u32[]{:S(2)}) collective-permute-start(bf16[3,64,128]{2,1,0:T(8,128)(2,1)S(1)} %get-tuple-element.62), channel_id=1, source_target_pairs={{0,7},{1,0},{2,1},{3,2},{4,3},{5,4},{6,5},{7,6},{8,15},{9,8},{10,9... | collective-permute-start | bytes 147464 | tf_op jit(solution)/shard_map/ppermute | solution.py:323
  20.2 4.7 %collective-permute-start.3 = (bf16[3,64,128]{2,1,0:T(8,128)(2,1)S(1)}, bf16[3,64,128]{2,1,0:T(8,128)(2,1)S(1)}, u32[]{:S(2)}, u32[]{:S(2)}) collective-permute-start(bf16[3,64,128]{2,1,0:T(8,128)(2,1)S(1)} %get-tuple-element.63), channel_id=1, source_target_pairs={{0,1},{1,2},{2,3},{3,4},{4,5},{5,6},{6,7},{7,0},{8,9},{9,10},{10,1... | collective-permute-start | bytes 147464 | tf_op jit(solution)/shard_map/ppermute | solution.py:323
  29.5 8.5 %collective-permute-start.4 = (bf16[1,8,8,128]{3,2,1,0:T(8,128)(2,1)S(1)}, bf16[1,8,8,128]{3,2,1,0:T(8,128)(2,1)S(1)}, u32[]{:S(2)}, u32[]{:S(2)}) collective-permute-start(bf16[1,8,8,128]{3,2,1,0:T(8,128)(2,1)S(1)} %get-tuple-element.58), channel_id=1, source_target_pairs={{0,8},{8,16},{16,24},{24,32},{32,40},{40,48},{48,56},{56,64},{64,7... | collective-permute-start | bytes 49160 | tf_op jit(solution)/shard_map/ppermute | solution.py:333
  29.6 8.4 %collective-permute-start.5 = (bf16[1,8,8,128]{3,2,1,0:T(8,128)(2,1)S(1)}, bf16[1,8,8,128]{3,2,1,0:T(8,128)(2,1)S(1)}, u32[]{:S(2)}, u32[]{:S(2)}) collective-permute-start(bf16[1,8,8,128]{3,2,1,0:T(8,128)(2,1)S(1)} %get-tuple-element.59), channel_id=1, source_target_pairs={{8,0},{16,8},{24,16},{32,24},{40,32},{48,40},{56,48},{64,56},{72,6... | collective-permute-start | bytes 49160 | tf_op jit(solution)/shard_map/ppermute | solution.py:334
  35.0 6.0 %collective-permute-start.10 = (bf16[34,1,4,8]{0,3,2,1:T(8,128)(2,1)S(1)}, bf16[34,1,4,8]{0,3,2,1:T(8,128)(2,1)S(1)}, u32[]{:S(2)}, u32[]{:S(2)}) collective-permute-start(bf16[34,1,4,8]{0,3,2,1:T(8,128)(2,1)S(1)} %get-tuple-element.60), channel_id=1, source_target_pairs={{0,1},{1,2},{2,3},{3,4},{4,5},{5,6},{6,7},{7,0},{8,9},{9,10},{10,1... | collective-permute-start | bytes 6536 | tf_op jit(solution)/shard_map/ppermute | solution.py:333
  35.1 6.0 %collective-permute-start.11 = (bf16[34,1,4,8]{0,3,2,1:T(8,128)(2,1)S(1)}, bf16[34,1,4,8]{0,3,2,1:T(8,128)(2,1)S(1)}, u32[]{:S(2)}, u32[]{:S(2)}) collective-permute-start(bf16[34,1,4,8]{0,3,2,1:T(8,128)(2,1)S(1)} %get-tuple-element.61), channel_id=1, source_target_pairs={{1,0},{2,1},{3,2},{4,3},{5,4},{6,5},{7,6},{0,7},{9,8},{10,9},{11,1... | collective-permute-start | bytes 6536 | tf_op jit(solution)/shard_map/ppermute | solution.py:334
  38.1 5.0 %collective-permute-start.6 = (bf16[34,1,8,128]{3,2,1,0:T(8,128)(2,1)S(1)}, bf16[34,1,8,128]{3,2,1,0:T(8,128)(2,1)S(1)}, u32[]{:S(2)}, u32[]{:S(2)}) collective-permute-start(bf16[34,1,8,128]{3,2,1,0:T(8,128)(2,1)S(1)} %get-tuple-element.56), channel_id=1, source_target_pairs={{0,1},{1,2},{2,3},{3,4},{4,5},{5,6},{6,7},{7,0},{8,9},{9,10},{10,1... | collective-permute-start | bytes 208904 | tf_op jit(solution)/shard_map/ppermute | solution.py:333
  38.1 4.9 %collective-permute-start.7 = (bf16[34,1,8,128]{3,2,1,0:T(8,128)(2,1)S(1)}, bf16[34,1,8,128]{3,2,1,0:T(8,128)(2,1)S(1)}, u32[]{:S(2)}, u32[]{:S(2)}) collective-permute-start(bf16[34,1,8,128]{3,2,1,0:T(8,128)(2,1)S(1)} %get-tuple-element.57), channel_id=1, source_target_pairs={{1,0},{2,1},{3,2},{4,3},{5,4},{6,5},{7,6},{0,7},{9,8},{10,9},{11,1... | collective-permute-start | bytes 208904 | tf_op jit(solution)/shard_map/ppermute | solution.py:334
  128.0 7.1 %collective-permute-start.12 = (bf16[10,8,128]{2,1,0:T(8,128)(2,1)S(1)}, bf16[10,8,128]{2,1,0:T(8,128)(2,1)S(1)}, u32[]{:S(2)}, u32[]{:S(2)}) collective-permute-start(bf16[10,8,128]{2,1,0:T(8,128)(2,1)S(1)} %fusion.9), channel_id=1, source_target_pairs={{0,8},{8,16},{16,24},{24,32},{32,40},{40,48},{48,56},{56,64},{64,7... | collective-permute-start | bytes 61448 | tf_op jit(solution)/shard_map/ppermute | solution.py:323
  137.2 3.8 %collective-permute-start.13 = (bf16[10,8,128]{2,1,0:T(8,128)(2,1)S(1)}, bf16[10,8,128]{2,1,0:T(8,128)(2,1)S(1)}, u32[]{:S(2)}, u32[]{:S(2)}) collective-permute-start(bf16[10,8,128]{2,1,0:T(8,128)(2,1)S(1)} %fusion.10), channel_id=1, source_target_pairs={{0,120},{8,0},{16,8},{24,16},{32,24},{40,32},{48,40},{56,48},{64,5... | collective-permute-start | bytes 61448 | tf_op jit(solution)/shard_map/ppermute | solution.py:323
  143.3 4.9 %collective-permute-start.14 = (bf16[32,8,128]{2,1,0:T(8,128)(2,1)S(1)}, bf16[32,8,128]{2,1,0:T(8,128)(2,1)S(1)}, u32[]{:S(2)}, u32[]{:S(2)}) collective-permute-start(bf16[32,8,128]{2,1,0:T(8,128)(2,1)S(1)} %fusion.4), channel_id=1, source_target_pairs={{0,1},{1,2},{2,3},{3,4},{4,5},{5,6},{6,7},{7,0},{8,9},{9,10},{10,1... | collective-permute-start | bytes 196616 | tf_op jit(solution)/shard_map/ppermute | solution.py:323
  144.8 6.5 %copy-start.2 = (bf16[128,128]{1,0:T(8,128)(2,1)S(1)}, bf16[128,128]{1,0:T(8,128)(2,1)}, u32[]{:S(2)}) copy-start(bf16[128,128]{1,0:T(8,128)(2,1)} %sw_ref.1) | copy-start | bytes 98308
  149.2 1.9 %collective-permute-start.15 = (bf16[32,8,128]{2,1,0:T(8,128)(2,1)S(1)}, bf16[32,8,128]{2,1,0:T(8,128)(2,1)S(1)}, u32[]{:S(2)}, u32[]{:S(2)}) collective-permute-start(bf16[32,8,128]{2,1,0:T(8,128)(2,1)S(1)} %fusion.5), channel_id=1, source_target_pairs={{0,7},{1,0},{2,1},{3,2},{4,3},{5,4},{6,5},{7,6},{8,15},{9,8},{10,9... | collective-permute-start | bytes 196616 | tf_op jit(solution)/shard_map/ppermute | solution.py:323
  151.1 1.2 copy-start
where the time goes:
time: 155 us; the launch traced here: 153 us
  Pallas kernels  83.1 us (54%)
  starting transfers between devices  24.9 us (16%)
  waiting for transfers between devices  22.9 us (15%)
  local copies, waits for them, and re-layouts  13.4 us (9%)
  other arithmetic  7.8 us (5%)
    pallas_call x1, Pallas kernels, edge_call(): pl.pallas_call(edge_kernel, out_shape=(jax.ShapeDtypeStruct((2048, 128),...  83.1 us
    ppermute x8, waiting for transfers between devices, shifted(): lax.ppermute(array, axis, [(i, (i + by) % size) for i in range(size)])  22 us
    ppermute x4, starting transfers between devices, extended(): after = lax.ppermute(first, axis, down)  16.6 us
    ppermute x8, starting transfers between devices, shifted(): lax.ppermute(array, axis, [(i, (i + by) % size) for i in range(size)])  8.11 us
    scatter x1, local copies, waits for them, and re-layouts, on_device(): flat_rows.at[target_slots]  4.54 us
  transfers between devices with their start and end apart: 16, of which 8 were waited for; matrix products, arithmetic and copies ran while one was open for 5% of the time, Pallas kernels for 0%

commit v1 on v0

--- a/solution.py
+++ b/solution.py
@@ -11,7 +11,9 @@
 BIG_PRE = 4096.0
 BIG_H = 131072.0
 NH = 18
-GROUP = 2
+MESH = pl.DeviceIdType.MESH
+DIRECTIONS = [k for k in range(9) if k != 4]
+GROUP = 8
 
 
 def mm(a, b):
@@ -40,11 +42,198 @@
     return n // 3, n % 3
 
 
+def neighbour(k):
+    dx, dy = step_of(k)
+    nx, ny = lax.axis_size("gx"), lax.axis_size("gy")
+    return (
+        lax.rem(lax.axis_index("gx") + (dx - 1 + nx), nx),
+        lax.rem(lax.axis_index("gy") + (dy - 1 + ny), ny),
+    )
+
+
+def greet():
+    barrier = pltpu.get_barrier_semaphore()
+    for k in DIRECTIONS:
+        pl.semaphore_signal(barrier, inc=1, device_id=neighbour(k), device_id_type=MESH)
+    pl.semaphore_wait(barrier, 8)
+
+
+def send(k, source, target, send_sem, recv_sem):
+    copy = pltpu.make_async_remote_copy(
+        src_ref=source, dst_ref=target, send_sem=send_sem.at[k], recv_sem=recv_sem.at[k],
+        device_id=neighbour(k), device_id_type=MESH,
+    )
+    copy.start()
+    return copy
+
+
+def rim_slot(k):
+    dx, dy = step_of(k)
+    if dy == 1:
+        return 0, dx // 2
+    if dx == 1:
+        return 1, dy // 2
+    return 2, dx // 2 * 2 + dy // 2
+
+
+def move_kernel(
+    lat_ref, leave_ref, land_ref, geo_ref,
+    rel_ref, hx_ref, hy_ref, hc_ref, gin_ref,
+    out_buf, in_buf, sx, sy, sc, tx, ty, tc, pick_ref, place_ref, cat_ref,
+    send1, recv1, send2, recv2,
+):
+    leave = leave_ref[...]
+    upper = jnp.where(leave < 0, -64, leave // 64 * 64)
+    lower = (leave - upper).astype(F32)
+    upper = upper.astype(F32)
+    eye = iota((64, 64), 0) == iota((64, 64), 1)
+    ones = jnp.ones((64, 128), BF)
+    slots = iota((64, 128), 1).astype(F32)
+    for k in range(9):
+        column = mm(jnp.where(eye, upper[k : k + 1], 0.0).astype(BF), ones) + mm(
+            jnp.where(eye, lower[k : k + 1], 0.0).astype(BF), ones
+        )
+        for t in range(16):
+            pick_ref[k * 64 : k * 64 + 64, t * 128 : t * 128 + 128] = jnp.where(
+                column == slots + t * 128.0, 1.0, 0.0
+            ).astype(BF)
+    picked = mm(pick_ref[...], lat_ref[...]).astype(BF)
+    edges = jnp.where(
+        iota((64, 256), 1) == iota((64, 256), 0) % 32 * 8 + iota((64, 256), 0) // 32 * 7, 1.0, 0.0
+    ).astype(BF)
+    geo_y = mm(edges, geo_ref[...]).astype(BF)
+    for k in range(9):
+        dx, dy = step_of(k)
+        out_buf[k, 0:64] = picked[k * 64 : k * 64 + 64]
+        if dx == 1 and dy != 1:
+            out_buf[k, 64:96] = geo_y[dy // 2 * 32 : dy // 2 * 32 + 32]
+        else:
+            first = 0 if dx == 0 else 224
+            out_buf[k, 64:96] = geo_ref[first : first + 32]
+    greet()
+    first = [send(k, out_buf.at[k], in_buf.at[k], send1, recv1) for k in DIRECTIONS]
+    land = land_ref[...]
+    for t in range(5):
+        if t < 4:
+            row = jnp.concatenate([land[2 * t : 2 * t + 1], land[2 * t + 1 : 2 * t + 2]], axis=1)
+        else:
+            row = jnp.concatenate([land[8:9], jnp.full((1, 64), -1, jnp.int32)], axis=1)
+        for u in range(8):
+            place_ref[u * 256 : u * 256 + 256, t * 128 : t * 128 + 128] = jnp.where(
+                iota((256, 128), 0) + u * 256 == row, 1.0, 0.0
+            ).astype(BF)
+    cat_ref[:, 128:256] = jnp.ones((640, 128), BF)
+    cat_ref[576:640, 0:128] = jnp.zeros((64, 128), BF)
+    cat_ref[256:320, 0:128] = picked[256:320]
+    for copy in first:
+        copy.wait()
+    for k in DIRECTIONS:
+        cat_ref[k * 64 : k * 64 + 64, 0:128] = in_buf[k, 0:64]
+        gin_ref[k] = in_buf[k, 64:96]
+    gin_ref[4] = jnp.zeros((32, 128), BF)
+    for u in range(4):
+        at = slice(u * 512, u * 512 + 512)
+        placed = mm(place_ref[at, :], cat_ref[...])
+        rows = lat_ref[at, :].astype(F32) * (1.0 - placed[:, 128:256]) + placed[:, 0:128]
+        rel_ref[at, :] = rows.astype(BF)
+        cells = rows.reshape(8, 8, 8, 128)
+        sy[0, u * 64 : u * 64 + 64] = cells[:, 0].reshape(64, 128).astype(BF)
+        sy[1, u * 64 : u * 64 + 64] = cells[:, 7].reshape(64, 128).astype(BF)
+        if u == 0:
+            sx[0] = rows[0:64].astype(BF)
+            sc[0] = rows[0:16].astype(BF)
+            sc[1] = rows[48:64].astype(BF)
+        if u == 3:
+            sx[1] = rows[448:512].astype(BF)
+            sc[2] = rows[448:464].astype(BF)
+            sc[3] = rows[496:512].astype(BF)
+    pairs = ((sx, tx), (sy, ty), (sc, tc))
+    second = []
+    for k in DIRECTIONS:
+        kind, place = rim_slot(k)
+        source, target = pairs[kind]
+        second.append(send(k, source.at[place], target.at[place], send2, recv2))
+    for copy in second:
+        copy.wait()
+    hx_ref[...] = tx[...]
+    hy_ref[...] = ty[...]
+    hc_ref[...] = tc[...]
+
+
+def move_call(latent, leaving, landing, geo):
+    full = pl.BlockSpec(memory_space=pltpu.VMEM)
+    rim = [(2, 64, 128), (2, 256, 128), (4, 16, 128)]
+    return pl.pallas_call(
+        move_kernel,
+        out_shape=[jax.ShapeDtypeStruct(s, BF) for s in [(2048, 128)] + rim + [(9, 32, 128)]],
+        in_specs=[full] * 4,
+        out_specs=[full] * 5,
+        scratch_shapes=[pltpu.VMEM((9, 96, 128), BF), pltpu.VMEM((9, 96, 128), BF)]
+        + [pltpu.VMEM(s, BF) for s in rim + rim]
+        + [
+            pltpu.VMEM((576, 2048), BF),
+            pltpu.VMEM((2048, 640), BF),
+            pltpu.VMEM((640, 256), BF),
+        ]
+        + [pltpu.SemaphoreType.DMA((9,))] * 4,
+        compiler_params=pltpu.CompilerParams(
+            collective_id=0, has_side_effects=True, vmem_limit_bytes=24 * 1024 * 1024
+        ),
+        name="move",
+    )(latent, leaving, landing, geo)
+
+
+def return_kernel(
+    grad_ref, rx_ref, ry_ref, rc_ref, sw_ref, out_ref, sx, sy, sc, tx, ty, tc, send_sem, recv_sem
+):
+    sx[...] = rx_ref[...]
+    sy[...] = ry_ref[...]
+    sc[...] = rc_ref[...]
+    greet()
+    pairs = ((sx, tx), (sy, ty), (sc, tc))
+    copies = []
+    for k in DIRECTIONS:
+        kind, place = rim_slot(k)
+        source, target = pairs[kind]
+        copies.append(send(k, source.at[place], target.at[place], send_sem, recv_sem))
+    out_ref[...] = grad_ref[...]
+    for copy in copies:
+        copy.wait()
+    sw = sw_ref[...]
+    for side in range(2):
+        at = 31 if side == 0 else 0
+        out_ref[at] += mmt(tx[side], sw).reshape(8, 8, 128)
+        at = 7 if side == 0 else 0
+        out_ref[:, at] += mmt(ty[side], sw).reshape(32, 8, 128)
+    corner = mmt(tc[...].reshape(64, 128), sw).reshape(4, 16, 128)[:, 0:8]
+    out_ref[31, 7] += corner[0]
+    out_ref[31, 0] += corner[1]
+    out_ref[0, 7] += corner[2]
+    out_ref[0, 0] += corner[3]
+
+
+def return_call(grad, rx, ry, rc, sender_weight):
+    full = pl.BlockSpec(memory_space=pltpu.VMEM)
+    rim = [(2, 64, 128), (2, 256, 128), (4, 16, 128)]
+    return pl.pallas_call(
+        return_kernel,
+        out_shape=jax.ShapeDtypeStruct((32, 8, 8, 128), F32),
+        in_specs=[full] * 5,
+        out_specs=full,
+        scratch_shapes=[pltpu.VMEM(s, BF) for s in rim + rim] + [pltpu.SemaphoreType.DMA((9,))] * 2,
+        compiler_params=pltpu.CompilerParams(
+            collective_id=1, has_side_effects=True, vmem_limit_bytes=24 * 1024 * 1024
+        ),
+        name="give_back",
+    )(grad, rx, ry, rc, sender_weight)
+
+
 def edge_kernel(
-    wl_ref, geom_ref, cot_ref, ew_ref, eb_ref, rw_ref, sw_ref, dw_ref, db_ref, mw_ref, mb_ref,
+    rel_ref, hx_ref, hy_ref, hc_ref, geo_ref, gin_ref, cot_ref,
+    ew_ref, eb_ref, rw_ref, sw_ref, dw_ref, db_ref, mw_ref, mb_ref,
     nw_ref, uw_ref, nb_ref, ow_ref, ob_ref, gain_ref,
-    upd_ref, grad_ref, send_ref,
-    gj_ref, gi_ref, s_ref, r_ref, rel_ref, occ_ref, cnt_ref, w1_ref, bd_ref,
+    upd_ref, grad_ref, rx_ref, ry_ref, rc_ref,
+    gj_ref, gi_ref, sf_ref, s_ref, r_ref, occ_ref, cc_ref, w1_ref, bd_ref,
     se_ref, sh_ref, sg_ref, pull_ref, acc_ref, g_ref,
 ):
     lane = iota((128, 128), 1)
@@ -83,39 +272,52 @@
     const_j = jnp.where((const_blk == 12) | (const_blk == 13), 1.0, 0.0) + jnp.where(
         const_blk == 14, -BIG_PRE, 0.0
     )
-    rep80 = jnp.where(iota((80, 16), 0) // 8 == iota((80, 16), 1), 1.0, 0.0).astype(BF)
-    own80 = iota((80, 128), 0) % 8 == iota((80, 128), 1) % 8
-    near = iota((64, 16), 1) - iota((64, 16), 0) // 8
-    band64 = jnp.where((near >= 0) & (near <= 2), 1.0, 0.0).astype(BF)
     sw_half = (sw_ref[...].astype(F32) * 0.5).astype(BF)
     rw_half = (rw_ref[...].astype(F32) * 0.5).astype(BF)
     eb_half = db_ref[...] * 0.5
 
-    def one_row(x):
-        slab = wl_ref[pl.ds(pl.multiple_of(x * 80, 16), 80), :]
-        geom = geom_ref[x]
-        rep = jnp.where(own80, mm(rep80, geom), 0.0).astype(BF)
+    def sender_rows(rows, cells, offset, count):
+        size = cells.shape[0]
+        spread = jnp.where(
+            iota((count * 8, size), 0) // 8 + offset == iota((count * 8, size), 1), 1.0, 0.0
+        ).astype(BF)
+        every = mm(spread, cells)
+        own = iota((count * 8, 128), 0) % 8 == iota((count * 8, 128), 1) % 8
+        rep = jnp.where(own, every, 0.0).astype(BF)
         gj = mm(rep, sel_j) + const_j
         occ = mm(rep, sel_o)
-        s = mm(slab, sw_half) + (occ * BIG_H - BIG_H)
-        return slab, geom, gj, occ, s
+        s = mm(rows, sw_half)[: count * 8] + (occ * BIG_H - BIG_H)
+        number = mm(every.astype(BF), sel_o)
+        return gj, s, number, occ
+
+    def fill(where, values, shape):
+        for table, value in zip((gj_ref, sf_ref, cc_ref), values):
+            table[where] = value.reshape(shape)
+
+    for u in range(4):
+        at = slice(u * 512, u * 512 + 512)
+        rows = rel_ref[at, :]
+        gj, s, number, occ = sender_rows(rows, geo_ref[u * 64 : u * 64 + 64], 0, 64)
+        fill((slice(1 + 8 * u, 9 + 8 * u), slice(1, 9)), (gj, s, number), (8, 8, 8, 128))
+        occ_ref[at, :] = occ
+        r_ref[at, :] = mm(rows, rw_half) + eb_half
+        gi_ref[u * 64 : u * 64 + 64] = mm(geo_ref[u * 64 : u * 64 + 64], sel_i)
+    for side in range(2):
+        k = 1 if side == 0 else 7
+        values = sender_rows(hx_ref[side], gin_ref[k], 0 if side == 0 else 24, 8)[:3]
+        fill((33 if side == 0 else 0, slice(1, 9)), values, (8, 8, 128))
+        k = 3 if side == 0 else 5
+        values = sender_rows(hy_ref[side], gin_ref[k], 0, 32)[:3]
+        fill((slice(1, 33), 9 if side == 0 else 0), values, (32, 8, 128))
+    for place, (k, first, x, y) in enumerate(((0, 0, 33, 9), (2, 7, 33, 0), (6, 24, 0, 9), (8, 31, 0, 0))):
+        rows = hc_ref[place]
+        gj, s, number, _ = sender_rows(rows, gin_ref[k], first - (first % 8 != 0), 2)
+        at = 8 if first % 8 else 0
+        fill((x, y), (gj[at : at + 8], s[at : at + 8], number[at : at + 8]), (8, 128))
 
     @pl.loop(0, NH)
     def _(x):
-        parts = [one_row(x), one_row(x + 16)]
-        gj_ref[x] = jnp.concatenate([v[2].reshape(10, 8, 128) for v in parts], axis=1)
-        s_ref[x] = jnp.concatenate([v[4].reshape(10, 8, 128) for v in parts], axis=1).astype(BF)
-
-    @pl.loop(0, 32)
-    def _(x):
-        slab, geom, _, occ, _ = one_row(x + 1)
-        at = pl.ds(pl.multiple_of(x * 64, 64), 64)
-        r_ref[at, :] = mm(slab, rw_half)[8:72] + eb_half
-        rel_ref[at, :] = slab.astype(F32)[8:72]
-        occ_ref[at, :] = occ[8:72]
-        gi_ref[x] = mm(geom, sel_i)
-        near_occ = geom_ref[x].astype(F32) + geom.astype(F32) + geom_ref[x + 2].astype(F32)
-        cnt_ref[at, :] = mm(mm(band64, near_occ.astype(BF)).astype(BF), sel_o) - 1.0
+        s_ref[x] = jnp.concatenate([sf_ref[x], sf_ref[x + 16]], axis=1).astype(BF)
 
     lane16 = iota((16, 128), 1)
     row16 = iota((16, 128), 0)
@@ -143,14 +345,17 @@
             y = y0 + c
             gi = jnp.concatenate(
                 [
-                    jnp.broadcast_to(gi_ref[x, pl.ds(y + 1, 1), :], (8, 128)),
-                    jnp.broadcast_to(gi_ref[x + 16, pl.ds(y + 1, 1), :], (8, 128)),
+                    jnp.broadcast_to(gi_ref[pl.ds(x * 8 + y, 1), :], (8, 128)),
+                    jnp.broadcast_to(gi_ref[pl.ds(x * 8 + y + 128, 1), :], (8, 128)),
                 ],
                 axis=0,
             )
             for n in range(9):
                 dx, dy = step_of(n)
-                reach = gj_ref[x + dx, y + dy] - gi
+                reach = (
+                    jnp.concatenate([gj_ref[x + dx, y + dy], gj_ref[x + 16 + dx, y + dy]], axis=0)
+                    - gi
+                )
                 if dx != 1 or dy != 1:
                     shift = jnp.where(
                         linear_c == 0, F32(dx - 1), jnp.where(linear_c == 1, F32(dy - 1), 0.0)
@@ -216,14 +421,18 @@
 
     @pl.loop(0, 2048 // CH)
     def _(k):
+        wide_x = CH // 64
+        near_y = cc_ref[pl.ds(k * wide_x, wide_x + 2)]
+        near_y = near_y[:, 0:8] + near_y[:, 1:9] + near_y[:, 2:10]
+        near = near_y[0:wide_x] + near_y[1 : wide_x + 1] + near_y[2 : wide_x + 2]
+        number = near.reshape(CH, 128) - 1.0
         at = pl.ds(pl.multiple_of(k * CH, CH), CH)
         sh = sh_ref[at, :]
         sh_b = sh.astype(BF)
         sh_l = (sh - sh_b.astype(F32)).astype(BF)
         mw = mw_ref[...]
-        summed = se_ref[at, :] + mm(sh_b, mw) + mm(sh_l, mw) + cnt_ref[at, :] * mb_ref[...]
-        rel = rel_ref[at, :]
-        inner = mm(rel.astype(BF), nw_ref[...]) + mm(summed.astype(BF), uw_ref[...]) + nb_ref[...]
+        summed = se_ref[at, :] + mm(sh_b, mw) + mm(sh_l, mw) + number * mb_ref[...]
+        inner = mm(rel_ref[at, :], nw_ref[...]) + mm(summed.astype(BF), uw_ref[...]) + nb_ref[...]
         h = inner * 0.5
         t = jnp.tanh(h)
         q = 1.0 + t
@@ -235,7 +444,7 @@
         normed = centred * inv
         occ = occ_ref[at, :]
         gain = gain_ref[...]
-        upd_ref[at, :] = (rel + occ * normed * gain).astype(BF)
+        upd_ref[at, :] = (rel_ref[at, :].astype(F32) + occ * normed * gain).astype(BF)
         cot = cot_ref[at, :].astype(F32)
         gn = occ * cot * gain
         go = (
@@ -276,34 +485,50 @@
             total = tree([g_ref[i, p, n] * pulls[p] for p in range(8)])
             acc_ref[x + dx, y + dy] += total.astype(F32)
 
-    for x in range(34):
+    def sent(x):
         if x < 16:
-            send_ref[x] = acc_ref[x, :, 0:8]
-        elif x < 18:
-            send_ref[x] = acc_ref[x, :, 0:8] + acc_ref[x - 16, :, 8:16]
-        else:
-            send_ref[x] = acc_ref[x - 16, :, 8:16]
-
-
-def edge_call(wl, geom, cot, *weights):
+            return acc_ref[x, :, 0:8]
+        if x < 18:
+            return acc_ref[x, :, 0:8] + acc_ref[x - 16, :, 8:16]
+        return acc_ref[x - 16, :, 8:16]
+
+    for u in range(4):
+        rows = [sent(1 + 8 * u + j) for j in range(8)]
+        core = jnp.concatenate([v[1:9].reshape(64, 128) for v in rows], axis=0).astype(BF)
+        at = slice(u * 512, u * 512 + 512)
+        grad_ref[at, :] += mmt(core, sw_ref[...])
+        for side in range(2):
+            rim = jnp.concatenate([v[9 * side] for v in rows], axis=0).astype(BF)
+            ry_ref[side, u * 64 : u * 64 + 64] = rim
+    for side in range(2):
+        row = sent(33 * side)
+        rx_ref[side] = row[1:9].reshape(64, 128).astype(BF)
+        for end in range(2):
+            cell = row[9 * end]
+            rc_ref[2 * side + end] = jnp.concatenate([cell, jnp.zeros_like(cell)], axis=0).astype(BF)
+
+
+def edge_call(*operands):
     full = pl.BlockSpec(memory_space=pltpu.VMEM)
     return pl.pallas_call(
         edge_kernel,
         out_shape=(
             jax.ShapeDtypeStruct((2048, 128), BF),
             jax.ShapeDtypeStruct((2048, 128), F32),
-            jax.ShapeDtypeStruct((34, 10, 8, 128), F32),
+            jax.ShapeDtypeStruct((2, 64, 128), BF),
+            jax.ShapeDtypeStruct((2, 256, 128), BF),
+            jax.ShapeDtypeStruct((4, 16, 128), BF),
         ),
-        in_specs=[full] * (3 + len(weights)),
-        out_specs=(full, full, full),
+        in_specs=[full] * len(operands),
+        out_specs=(full,) * 5,
         scratch_shapes=[
-            pltpu.VMEM((NH, 10, 16, 128), F32),
-            pltpu.VMEM((32, 16, 128), F32),
+            pltpu.VMEM((34, 10, 8, 128), F32),
+            pltpu.VMEM((256, 128), F32),
+            pltpu.VMEM((34, 10, 8, 128), F32),
             pltpu.VMEM((NH, 10, 16, 128), BF),
             pltpu.VMEM((2048, 128), F32),
             pltpu.VMEM((2048, 128), F32),
-            pltpu.VMEM((2048, 128), F32),
-            pltpu.VMEM((2048, 128), F32),
+            pltpu.VMEM((34, 10, 8, 128), F32),
             pltpu.VMEM((128, 1024), BF),
             pltpu.VMEM((256, 256), BF),
             pltpu.VMEM((2048, 128), F32),
@@ -315,25 +540,7 @@
         ],
         compiler_params=pltpu.CompilerParams(vmem_limit_bytes=62 * 1024 * 1024),
         name="edges",
-    )(wl, geom, cot, *weights)
-
-
-def shifted(array, axis, by):
-    size = lax.axis_size(axis)
-    return lax.ppermute(array, axis, [(i, (i + by) % size) for i in range(size)])
-
-
-def extended(array, sides, width):
-    for axis, dim in sides:
-        size, length = (lax.axis_size(axis), array.shape[dim])
-        up = [(i, (i + 1) % size) for i in range(size)]
-        down = [(j, i) for i, j in up]
-        last = lax.slice_in_dim(array, length - width, length, axis=dim)
-        first = lax.slice_in_dim(array, 0, width, axis=dim)
-        before = lax.ppermute(last, axis, up)
-        after = lax.ppermute(first, axis, down)
-        array = jnp.concatenate([before, array, after], axis=dim)
-    return array
+    )(*operands)
 
 
 def on_device(
@@ -341,60 +548,21 @@
     receiver_weight, sender_weight, edge_weight, edge_bias, message_weight, message_bias,
     node_weight, summed_weight, node_bias, output_weight, output_bias, norm_gain,
 ):
-    rows_x, width_y, slot_count, latent_width = latent.shape
-    slot_total = rows_x * width_y * slot_count
-    capacity = leaving.shape[3]
-    flat_rows = latent.reshape(slot_total, latent_width)
-    depart = leaving.reshape(9, capacity)
-    arrive = landing.reshape(9, capacity)
-    picked = flat_rows[jnp.clip(depart, 0, slot_total - 1)]
-    picked = jnp.where((depart >= 0)[..., None], picked, jnp.zeros_like(picked))
-    grouped = picked.reshape(3, 3, capacity, latent_width)
-    along_x = [None, grouped[1], None]
-    for step_by in (1, -1):
-        along_x[step_by + 1] = shifted(grouped[step_by + 1], "gx", step_by)
-    half_moved = jnp.stack(along_x, axis=0)
-    along_y = [None, half_moved[:, 1], None]
-    for step_by in (1, -1):
-        along_y[step_by + 1] = shifted(half_moved[:, step_by + 1], "gy", step_by)
-    arrived = jnp.stack(along_y, axis=1).reshape(9, capacity, latent_width)
-    target_slots = jnp.where(arrive >= 0, arrive, slot_total).reshape(-1)
-    relocated = flat_rows.at[target_slots].set(arrived.reshape(-1, latent_width), mode="drop")
-    relocated = relocated.reshape(rows_x, width_y, slot_count, latent_width)
-    occupied = (jnp.arange(slot_count)[None, None, :] < counts[:, :, None]).astype(BF)
-    geometry = jnp.concatenate([position, occupied[:, :, None, :]], axis=2)
-    wide_latent = extended(relocated, (("gx", 0), ("gy", 1)), 1)
-    wide_geometry = extended(geometry, (("gx", 0), ("gy", 1)), 1)
-    wide_geometry = jnp.pad(wide_geometry.reshape(34, 10, 32), ((0, 0), (0, 6), (0, 96)))
+    occupied = (jnp.arange(8)[None, :] < counts.reshape(256, 1)).astype(BF)
+    geo = jnp.concatenate([position.reshape(256, 24), occupied], axis=1)
+    geo = jnp.pad(geo, ((0, 0), (0, 96)))
+    relocated, hx, hy, hc, gin = move_call(
+        latent.reshape(2048, 128), leaving.reshape(9, 64), landing.reshape(9, 64), geo
+    )
     line = lambda v: v.reshape(1, -1)
-    updated, grad, folded = edge_call(
-        wide_latent.reshape(-1, latent_width), wide_geometry,
-        cotangent.reshape(slot_total, latent_width), encoder_weight, line(encoder_bias),
-        receiver_weight, sender_weight, edge_weight, line(edge_bias), message_weight,
-        line(message_bias), node_weight, summed_weight, line(node_bias), output_weight,
-        line(output_bias), line(norm_gain),
+    updated, grad, rx, ry, rc = edge_call(
+        relocated, hx, hy, hc, geo, gin, cotangent.reshape(2048, 128), encoder_weight,
+        line(encoder_bias), receiver_weight, sender_weight, edge_weight, line(edge_bias),
+        message_weight, line(message_bias), node_weight, summed_weight, line(node_bias),
+        output_weight, line(output_bias), line(norm_gain),
     )
-    for step_by in (1, -1):
-        edge_row = folded[rows_x + 1] if step_by == 1 else folded[0]
-        incoming = shifted(edge_row.astype(jnp.bfloat16), "gx", step_by).astype(edge_row.dtype)
-        if step_by == 1:
-            folded = folded.at[1].add(incoming)
-        else:
-            folded = folded.at[rows_x].add(incoming)
-    middle_rows = folded[1 : rows_x + 1]
-    for step_by in (1, -1):
-        column = middle_rows[:, width_y + 1] if step_by == 1 else middle_rows[:, 0]
-        incoming = shifted(column.astype(jnp.bfloat16), "gy", step_by).astype(column.dtype)
-        if step_by == 1:
-            middle_rows = middle_rows.at[:, 1].add(incoming)
-        else:
-            middle_rows = middle_rows.at[:, width_y].add(incoming)
-    send_core = middle_rows[:, 1 : width_y + 1]
-    grad = grad + lax.dot_general(
-        send_core.astype(BF).reshape(slot_total, latent_width), sender_weight,
-        (((1,), (1,)), ((), ())), preferred_element_type=F32,
-    )
-    return updated.reshape(latent.shape), grad.reshape(latent.shape)
+    grad = return_call(grad.reshape(latent.shape), rx, ry, rc, sender_weight)
+    return updated.reshape(latent.shape), grad
 
 
 def solution(mesh):

time: 155 us -> 93.3 us (0.60)
  starting transfers between devices: 24.9 us -> 0 us
  waiting for transfers between devices: 22.9 us -> 0 us
  other arithmetic: 7.8 us -> 0.01 us
  local copies, waits for them, and re-layouts: 13.4 us -> 10 us
    pallas_call x1, Pallas kernels: 83.1 us -> 50.4 us  [edge_call(): pl.pallas_call(edge_kernel, out_shape=(jax.ShapeDtypeStruct((2048, 128),...]
    pallas_call x0 -> x2, Pallas kernels: none -> 31.8 us  [the longest x1 22.2 us: move_call(): pl.pallas_call(move_kernel, out_shape=[jax.ShapeDtypeStruct(s, BF) for s...]
    ppermute x16 -> x0, starting transfers between devices: 24.9 us -> none  [the longest x4 16.6 us: extended(): after = lax.ppermute(first, axis, down)]
    ppermute x16 -> x0, waiting for transfers between devices: 22.9 us -> none  [the longest x8 22 us: shifted(): lax.ppermute(array, axis, [(i, (i + by) % size) for i in range(size)])]
    unnamed x12 -> x30, local copies, waits for them, and re-layouts: 1.86 us -> 9.55 us
    scatter x1 -> x0, local copies, waits for them, and re-layouts: 4.54 us -> none  [on_device(): flat_rows.at[target_slots]]
    scatter-add x4 -> x0, other arithmetic: 3.73 us -> none  [the longest x1 1.4 us: on_device(): folded = folded.at[1].add(incoming)]
    convert_element_type x4 -> x0, local copies, waits for them, and re-layouts: 2.49 us -> none  [the longest x2 1.56 us: on_device(): edge_row.astype(jnp.bfloat16)]
  transfers between devices with their start and end apart: 16 -> 0, of which waited for: 8 -> 0; matrix products, arithmetic and copies ran while one was open for 5% -> 0% of each run, Pallas kernels for 0% -> 0%
where the time goes in v1:
time: 93.3 us; the launch traced here: 92.9 us
  Pallas kernels  82.2 us (88%)
  local copies, waits for them, and re-layouts  10 us (11%)
    pallas_call x1, Pallas kernels, edge_call(): pl.pallas_call(edge_kernel, out_shape=(jax.ShapeDtypeStruct((2048, 128),...  50.4 us
    pallas_call x1, Pallas kernels, move_call(): pl.pallas_call(move_kernel, out_shape=[jax.ShapeDtypeStruct(s, BF) for s...  22.2 us
    pallas_call x1, Pallas kernels, return_call(): pl.pallas_call(return_kernel, out_shape=jax.ShapeDtypeStruct((32, 8, 8, 1...  9.61 us
    unnamed x30, local copies, waits for them, and re-layouts  9.55 us

profile of v1, /device:TPU:0, one launch (start us, length us, event | category | flops | bytes accessed | tf_op | source)
XLA Modules:
  0.0 92.9 jit_solution(6135917251539202558)
XLA Ops:
  0.6 0.0 copy-start.12
  0.6 0.0 copy-start.2
  0.6 0.8 copy.27
  1.5 0.1 lt.16
  1.6 0.7 copy_bitcast_fusion
  2.3 0.0 copy-done.12
  2.3 0.2 copy.26
  2.4 0.2 reshape.48
  2.7 0.1 copy.28
  2.8 0.0 copy-done.2
  2.9 0.0 copy-start.1
  2.9 22.2 %move.1 = (bf16[2048,128]{1,0:T(8,128)(2,1)S(1)}, bf16[2,64,128]{2,1,0:T(8,128)(2,1)S(1)}, bf16[2,256,128]{2,1,0:T(8,128)(2,1)S(1)}, bf16[4,16,128]{2,1,0:T(8,128)(2,1)S(1)}, bf16[9,32,128]{2,1,0:T(8,128)(2,1)S(1)}) custom-call(bf16[2048,128]{1,0:T(8,128)(2,1)S(1)} %bitcast.19, s32[9,64]{1,0:T(8,128)S(1)} %get-tuple-element.23.leave_ref, ...), custom_call_target="tpu_custom_call" | custom-call | tf_op jit(solution)/shard_map/move/pallas_call | solution.py:166
  25.1 0.0 copy-done.1
  25.1 0.0 copy-start.3
  25.1 0.8 copy-done.3
  25.9 0.0 copy-start.6
  25.9 0.6 copy-done.6
  26.5 0.0 copy-start.7
  26.5 0.6 copy-done.7
  27.1 0.0 copy-start.9
  27.2 0.6 copy-done.9
  27.8 0.0 copy-start.10
  27.8 0.6 copy-done.10
  28.4 0.0 copy-start.4
  28.4 50.4 %edges.1 = (bf16[2048,128]{1,0:T(8,128)(2,1)}, f32[2048,128]{1,0:T(8,128)}, bf16[2,64,128]{2,1,0:T(8,128)(2,1)}, bf16[2,256,128]{2,1,0:T(8,128)(2,1)}, bf16[4,16,128]{2,1,0:T(8,128)(2,1)}) custom-call(bf16[2048,128]{1,0:T(8,128)(2,1)} %copy-done.3, bf16[2,64,128]{2,1,0:T(8,128)(2,1)} %copy-done.9, bf16[2,256,128]{2,1,0:T(8,128)(2,1)} %copy-done.6, ...), custom_call_target="tpu_custom_call" | custom-call | tf_op jit(solution)/shard_map/edges/pallas_call | solution.py:513
  78.7 0.0 copy-done.4
  78.7 0.0 copy-start
  78.7 1.2 %copy-done = f32[2048,128]{1,0:T(8,128)S(1)} copy-done((f32[2048,128]{1,0:T(8,128)S(1)}, f32[2048,128]{1,0:T(8,128)}, u32[]{:S(2)}) %copy-start) | copy-done | bytes 1048600
  80.0 0.0 copy-start.5
  80.0 0.9 copy-done.5
  80.9 0.0 copy-start.8
  80.9 0.8 copy-done.8
  81.6 0.0 copy-start.11
  81.6 0.7 copy-done.11
  82.3 9.6 %give_back.1 = f32[32,8,8,128]{3,2,1,0:T(8,128)S(1)} custom-call(f32[32,8,8,128]{3,2,1,0:T(8,128)S(1)} %bitcast.18, bf16[2,64,128]{2,1,0:T(8,128)(2,1)S(1)} %copy-done.8, bf16[2,256,128]{2,1,0:T(8,128)(2,1)S(1)} %copy-done.5, bf16[4,16,128]{2,1,0:T(8,128)(2,1)S(1)} %copy-done.11, bf16[128,128]{1,0:T(8,128)(2,1)S(1)} %copy-done.4), custom_call_target="tpu_custom_call" | custom-call | tf_op jit(solution)/shard_map/give_back/pallas_call | solution.py:218
  92.0 1.0 %copy.34 = f32[32,8,8,128]{3,2,1,0:T(8,128)} copy(f32[32,8,8,128]{3,2,1,0:T(8,128)S(1)} %give_back.1) | data formatting | bytes 2097152
  (3 shorter events, 0.0 us)
Async XLA Ops:
  0.6 1.7 %copy-start.12 = (bf16[32,8,3,8]{0,3,2,1:T(8,128)(2,1)S(1)}, bf16[32,8,3,8]{0,3,2,1:T(8,128)(2,1)}, u32[]{:S(2)}) copy-start(bf16[32,8,3,8]{0,3,2,1:T(8,128)(2,1)} %param.21) | copy-start | bytes 36868
  0.6 2.2 %copy-start.2 = (bf16[32,8,8,128]{3,2,1,0:T(8,128)(2,1)S(1)}, bf16[32,8,8,128]{3,2,1,0:T(8,128)(2,1)}, u32[]{:S(2)}) copy-start(bf16[32,8,8,128]{3,2,1,0:T(8,128)(2,1)} %param.20) | copy-start | bytes 1572868
  2.9 22.2 %copy-start.1 = (bf16[256,128]{1,0:T(8,128)(2,1)}, bf16[256,128]{1,0:T(8,128)(2,1)S(1)}, u32[]{:S(2)}) copy-start(bf16[256,128]{1,0:T(8,128)(2,1)S(1)} %pad.4.geo_ref) | copy-start | bytes 196612
  25.1 0.8 copy-start.3
  25.9 0.6 copy-start.6
  26.5 0.6 copy-start.7
  27.1 0.6 copy-start.9
  27.8 0.6 copy-start.10
  28.4 50.4 %copy-start.4 = (bf16[128,128]{1,0:T(8,128)(2,1)S(1)}, bf16[128,128]{1,0:T(8,128)(2,1)}, u32[]{:S(2)}) copy-start(bf16[128,128]{1,0:T(8,128)(2,1)} %sw_ref.3) | copy-start | bytes 98308
  78.7 1.2 %copy-start = (f32[2048,128]{1,0:T(8,128)S(1)}, f32[2048,128]{1,0:T(8,128)}, u32[]{:S(2)}) copy-start(f32[2048,128]{1,0:T(8,128)} %get-tuple-element.18) | copy-start | bytes 3145732
  80.0 0.9 copy-start.5
  80.9 0.8 copy-start.8
  81.6 0.7 copy-start.11

commit v2 on v1

v2 whole, which is shorter than its diff:
```python
import jax
import jax.numpy as jnp
from jax import lax
from jax.experimental import pallas as pl
from jax.experimental.pallas import tpu as pltpu
from jax.sharding import PartitionSpec as P

ln_eps = 1e-05
F32 = jnp.float32
BF = jnp.bfloat16
BIG_PRE = 4096.0
BIG_H = 131072.0
NH = 18
MESH = pl.DeviceIdType.MESH
DIRECTIONS = [k for k in range(9) if k != 4]


def mm(a, b):
    return jnp.dot(a, b, preferred_element_type=F32)


def mmt(a, b):
    return lax.dot_general(a, b, (((1,), (1,)), ((), ())), preferred_element_type=F32)


def iota(shape, dim):
    return lax.broadcasted_iota(jnp.int32, shape, dim)


def tree(parts):
    parts = list(parts)
    while len(parts) > 1:
        parts = [
            parts[i] + parts[i + 1] if i + 1 < len(parts) else parts[i]
            for i in range(0, len(parts), 2)
        ]
    return parts[0]


def step_of(n):
    return n // 3, n % 3


def neighbour(k):
    dx, dy = step_of(k)
    nx, ny = lax.axis_size("gx"), lax.axis_size("gy")
    return (
        lax.rem(lax.axis_index("gx") + (dx - 1 + nx), nx),
        lax.rem(lax.axis_index("gy") + (dy - 1 + ny), ny),
    )


def send(k, source, target, send_sem, recv_sem):
    copy = pltpu.make_async_remote_copy(
        src_ref=source, dst_ref=target, send_sem=send_sem.at[k], recv_sem=recv_sem.at[k],
        device_id=neighbour(k), device_id_type=MESH,
    )
    copy.start()
    return copy


def rim_slot(k):
    dx, dy = step_of(k)
    if dy == 1:
        return 0, dx // 2
    if dx == 1:
        return 1, dy // 2
    return 2, dx // 2 * 2 + dy // 2


def step_kernel(
    lat_ref, leave_ref, land_ref, geo_ref, cot_ref,
    ew_ref, eb_ref, rw_ref, sw_ref, dw_ref, db_ref, mw_ref, mb_ref,
    nw_ref, uw_ref, nb_ref, ow_ref, ob_ref, gain_ref,
    upd_ref, grad_ref,
    out_buf, in_buf, sx, sy, sc, tx, ty, tc, bx, by, bc, dx_buf, dy_buf, dc_buf,
    hot_ref, cat_ref, rel_ref,
    gj_ref, gi_ref, sf_ref, s_ref, r_ref, occ_ref, cc_ref, w1_ref, bd_ref, red_ref,
    se_ref, sh_ref, sg_ref, g_ref,
    send1, recv1, send2, recv2, send3, recv3,
):
    barrier = pltpu.get_barrier_semaphore()
    for k in DIRECTIONS:
        pl.semaphore_signal(barrier, inc=1, device_id=neighbour(k), device_id_type=MESH)
    leave = leave_ref[...]
    upper = jnp.where(leave < 0, -64, leave // 64 * 64)
    lower = (leave - upper).astype(F32)
    upper = upper.astype(F32)
    eye = iota((64, 64), 0) == iota((64, 64), 1)
    ones = jnp.ones((64, 128), BF)
    slots = iota((64, 128), 1).astype(F32)
    for k in range(9):
        column = mm(jnp.where(eye, upper[k : k + 1], 0.0).astype(BF), ones) + mm(
            jnp.where(eye, lower[k : k + 1], 0.0).astype(BF), ones
        )
        for t in range(16):
            row = t // 4 * 576 + k * 64
            hot_ref[row : row + 64, t % 4 * 128 : t % 4 * 128 + 128] = jnp.where(
                column == slots + t * 128.0, 1.0, 0.0
            ).astype(BF)
    picked = tree(
        [
            mm(hot_ref[u * 576 : u * 576 + 576, 0:512], lat_ref[u * 512 : u * 512 + 512, :])
            for u in range(4)
        ]
    ).astype(BF)
    edges = jnp.where(
        iota((64, 256), 1) == iota((64, 256), 0) % 32 * 8 + iota((64, 256), 0) // 32 * 7, 1.0, 0.0
    ).astype(BF)
    geo_y = mm(edges, geo_ref[...]).astype(BF)
    for k in range(9):
        dx, dy = step_of(k)
        out_buf[k, 0:64] = picked[k * 64 : k * 64 + 64]
        if dx == 1 and dy != 1:
            out_buf[k, 64:96] = geo_y[dy // 2 * 32 : dy // 2 * 32 + 32]
        else:
            first = 0 if dx == 0 else 224
            out_buf[k, 64:96] = geo_ref[first : first + 32]
    pl.semaphore_wait(barrier, 8)
    first = [send(k, out_buf.at[k], in_buf.at[k], send1, recv1) for k in DIRECTIONS]
    land = land_ref[...]
    for t in range(5):
        if t < 4:
            row = jnp.concatenate([land[2 * t : 2 * t + 1], land[2 * t + 1 : 2 * t + 2]], axis=1)
        else:
            row = jnp.concatenate([land[8:9], jnp.full((1, 64), -1, jnp.int32)], axis=1)
        for u in range(8):
            hot_ref[u * 256 : u * 256 + 256, t * 128 : t * 128 + 128] = jnp.where(
                iota((256, 128), 0) + u * 256 == row, 1.0, 0.0
            ).astype(BF)
    cat_ref[:, 128:256] = jnp.ones((640, 128), BF)
    cat_ref[576:640, 0:128] = jnp.zeros((64, 128), BF)
    cat_ref[256:320, 0:128] = picked[256:320]
    lane = iota((128, 128), 1)
    row = iota((128, 128), 0)
    whole = ew_ref[...]
    high = whole.astype(BF).astype(F32)
    low = whole - high
    bias_high = eb_ref[...].astype(BF).astype(F32)
    bias_low = eb_ref[...] - bias_high
    wide = lambda v: jnp.broadcast_to(v, (8, 128))
    blocks = [wide(high[c : c + 1]) for c in range(3)]
    blocks += [wide(low[c : c + 1]) for c in range(3)]
    blocks += [wide(high[3:4])] * 3 + [wide(low[3:4])] * 3
    blocks += [wide(bias_high), wide(bias_low)]
    blocks += [jnp.ones((16, 128), F32)]
    stacked = jnp.concatenate(blocks, axis=0)
    for p in range(8):
        w1_ref[:, p * 128 : (p + 1) * 128] = jnp.where(row % 8 == p, stacked, 0.0).astype(BF)
    half_w = (dw_ref[...].astype(F32) * 0.5).astype(BF)
    bd_ref[...] = jnp.zeros((256, 256), BF)
    bd_ref[0:128, 0:128] = half_w
    bd_ref[128:256, 128:256] = half_w

    comp = row // 8
    slot = row % 8
    blk = lane // 8
    in_p = lane % 8
    is_pos = blk < 12
    sel_j = jnp.where(
        is_pos & (comp == blk % 3), 1.0, 0.0
    ) + jnp.where((blk == 14) & (comp == 3), BIG_PRE, 0.0)
    sel_j = jnp.where(comp < 4, sel_j, 0.0).astype(BF)
    sel_i = jnp.where(is_pos & (comp == blk % 3) & (slot == in_p), 1.0, 0.0).astype(BF)
    sel_o = jnp.where(comp == 3, 1.0, 0.0).astype(BF)
    const_blk = iota((1, 128), 1) // 8
    const_j = jnp.where((const_blk == 12) | (const_blk == 13), 1.0, 0.0) + jnp.where(
        const_blk == 14, -BIG_PRE, 0.0
    )
    sw_half = (sw_ref[...].astype(F32) * 0.5).astype(BF)
    rw_half = (rw_ref[...].astype(F32) * 0.5).astype(BF)
    eb_half = db_ref[...] * 0.5

    red_row = iota((128, 1024), 0)
    red_col = iota((128, 1024), 1)
    red_ref[...] = jnp.where(
        (red_row // 64 == red_col // 8 % 2)
        & (red_row // 8 % 8 == red_col // 16 % 8)
        & (red_row % 8 == red_col // 128),
        1.0,
        0.0,
    ).astype(BF)

    def cell_rows(cells, offset, count):
        size = cells.shape[0]
        lift = jnp.where(
            iota((count * 8, size), 0) // 8 + offset == iota((count * 8, size), 1), 1.0, 0.0
        ).astype(BF)
        every = mm(lift, cells).astype(BF)
        own = iota((count * 8, 128), 0) % 8 == iota((count * 8, 128), 1) % 8
        rep = jnp.where(own, every.astype(F32), 0.0).astype(BF)
        occ = mm(rep, sel_o)
        return mm(rep, sel_j) + const_j, occ * BIG_H - BIG_H, mm(every, sel_o), occ, every

    def fill(where, values, shape):
        for table, value in zip((gj_ref, sf_ref, cc_ref), values):
            table[where] = value.reshape(shape)

    for u in range(4):
        at = slice(u * 512, u * 512 + 512)
        gj, mask, number, occ, every = cell_rows(geo_ref[u * 64 : u * 64 + 64], 0, 64)
        cells = slice(8 * u, 8 * u + 8)
        fill((slice(1 + 8 * u, 9 + 8 * u), slice(1, 9)), (gj, mask, number), (8, 8, 8, 128))
        occ_ref[at, :] = occ
        gi_ref[cells] = mm(every, sel_i).reshape(8, 8, 8, 128)
    for copy in first:
        copy.wait()
    for k in DIRECTIONS:
        cat_ref[k * 64 : k * 64 + 64, 0:128] = in_buf[k, 0:64]
    for u in range(4):
        at = slice(u * 512, u * 512 + 512)
        placed = mm(hot_ref[at, :], cat_ref[...])
        rows = lat_ref[at, :].astype(F32) * (1.0 - placed[:, 128:256]) + placed[:, 0:128]
        rel_ref[at, :] = rows.astype(BF)
        cells = rows.reshape(8, 8, 8, 128)
        sy[0, u * 64 : u * 64 + 64] = cells[:, 0].reshape(64, 128).astype(BF)
        sy[1, u * 64 : u * 64 + 64] = cells[:, 7].reshape(64, 128).astype(BF)
        if u == 0:
            sx[0] = rows[0:64].astype(BF)
            sc[0] = rows[0:16].astype(BF)
            sc[1] = rows[48:64].astype(BF)
        if u == 3:
            sx[1] = rows[448:512].astype(BF)
            sc[2] = rows[448:464].astype(BF)
            sc[3] = rows[496:512].astype(BF)
    pairs = ((sx, tx), (sy, ty), (sc, tc))
    second = []
    for k in DIRECTIONS:
        kind, place = rim_slot(k)
        source, target = pairs[kind]
        second.append(send(k, source.at[place], target.at[place], send2, recv2))
    for side in range(2):
        k = 1 if side == 0 else 7
        values = cell_rows(in_buf[k, 64:96], 0 if side == 0 else 24, 8)[:3]
        fill((33 if side == 0 else 0, slice(1, 9)), values, (8, 8, 128))
        k = 3 if side == 0 else 5
        values = cell_rows(in_buf[k, 64:96], 0, 32)[:3]
        fill((slice(1, 33), 9 if side == 0 else 0), values, (32, 8, 128))
    corners = ((0, 0, 33, 9), (2, 7, 33, 0), (6, 24, 0, 9), (8, 31, 0, 0))
    for k, first_row, x, y in corners:
        odd = first_row % 8 != 0
        values = cell_rows(in_buf[k, 64:96], first_row - odd, 2)[:3]
        at = 8 if odd else 0
        fill((x, y), [v[at : at + 8] for v in values], (8, 128))
    for u in range(4):
        rows = rel_ref[u * 512 : u * 512 + 512, :]
        cells = slice(8 * u, 8 * u + 8)
        sf_ref[1 + 8 * u : 9 + 8 * u, 1:9] += mm(rows, sw_half).reshape(8, 8, 8, 128)
        r_ref[cells] = (mm(rows, rw_half) + eb_half).reshape(8, 8, 8, 128)
    for copy in second:
        copy.wait()
    for side in range(2):
        x = 33 if side == 0 else 0
        sf_ref[x, 1:9] += mm(tx[side], sw_half).reshape(8, 8, 128)
        y = 9 if side == 0 else 0
        sf_ref[1:33, y] += mm(ty[side], sw_half).reshape(32, 8, 128)
    for place, (k, first_row, x, y) in enumerate(corners):
        at = 8 if first_row % 8 else 0
        sf_ref[x, y] += mm(tc[place], sw_half)[at : at + 8]

    @pl.loop(0, NH)
    def _(x):
        s_ref[x] = jnp.concatenate([sf_ref[x], sf_ref[x + 16]], axis=1).astype(BF)

    tile = (8, 16, 128)
    blk16 = iota(tile, 2) // 8
    squared = (blk16 >= 6) & (blk16 < 12)
    linear_c = jnp.where(blk16 < 12, blk16 % 3, 3)
    eye = jnp.where((blk16 == 15) & (iota(tile, 2) % 8 == iota(tile, 1) % 8), -BIG_PRE, 0.0)
    def both(ref, x):
        return jnp.concatenate([ref[x], ref[x + 16]], axis=1)

    def spread(rows, p):
        return jnp.concatenate(
            [jnp.broadcast_to(v[:, p : p + 1], (8, 8, 128)) for v in rows], axis=1
        ).reshape(128, 128)

    @pl.loop(0, 16)
    def _(x):
        gi = both(gi_ref, x)
        feats = []
        for n in range(9):
            dx, dy = step_of(n)
            reach = (
                jnp.concatenate(
                    [gj_ref[x + dx, dy : dy + 8], gj_ref[x + 16 + dx, dy : dy + 8]], axis=1
                )
                - gi
            )
            if n != 4:
                reach = reach + jnp.where(
                    linear_c == 0, float(dx - 1), jnp.where(linear_c == 1, float(dy - 1), 0.0)
                )
            value = jnp.where(squared, reach * reach, reach)
            if n == 4:
                value = value + eye
            feats.append(value.reshape(128, 128).astype(BF))
        feats = jnp.concatenate(feats, axis=0)
        own_rows = (r_ref[x], r_ref[x + 16])
        parts = [[], [], []]
        for pp in range(4):
            pre = mm(feats, w1_ref[:, pp * 256 : (pp + 1) * 256])
            enc = jnp.maximum(pre.astype(BF), BF(0))
            hh = mm(enc, bd_ref[...]).astype(BF)
            for half in range(2):
                p = 2 * pp + half
                cols = slice(half * 128, half * 128 + 128)
                r = spread(own_rows, p).astype(BF)
                pieces = [[], [], []]
                for y in range(0, 8, 2):
                    stacks = [[], [], []]
                    inside = slice(y * 16, (y + 2) * 16)
                    for n in range(9):
                        dx, dy = step_of(n)
                        at = slice(n * 128 + y * 16, n * 128 + (y + 2) * 16)
                        near = s_ref[x + dx, dy + y : dy + y + 2].reshape(32, 128)
                        h = hh[at, cols] + (near + r[inside])
                        if n == 4:
                            own = iota((32, 128), 0) % 8 == p
                            h = h + jnp.where(own, -BIG_H, 0.0).astype(BF)
                        t = jnp.tanh(h)
                        q = BF(1) + t
                        silu = h * q
                        slope = q + silu * (BF(1) - t)
                        g_ref[x, p, n, inside] = slope
                        for stack, value in zip(stacks, (enc[at, cols], silu, slope)):
                            stack.append((1, value))
                            while len(stack) > 1 and (stack[-1][0] == stack[-2][0] or n == 8):
                                last, before = stack.pop(), stack.pop()
                                stack.append((last[0] + before[0], last[1] + before[1]))
                    for piece, stack in zip(pieces, stacks):
                        piece.append(stack[0][1])
                for part, piece in zip(parts, pieces):
                    part.append(jnp.concatenate(piece, axis=0))
        for part, out in zip(parts, (se_ref, sh_ref, sg_ref)):
            total = mm(red_ref[...], jnp.concatenate(part, axis=0))
            at = pl.multiple_of(x * 64, 64)
            out[pl.ds(at, 64), :] = total[:64]
            out[pl.ds(at + 1024, 64), :] = total[64:]

    CH = 512

    @pl.loop(0, 2048 // CH)
    def _(k):
        wide_x = CH // 64
        near_y = cc_ref[pl.ds(k * wide_x, wide_x + 2)]
        near_y = near_y[:, 0:8] + near_y[:, 1:9] + near_y[:, 2:10]
        near = near_y[0:wide_x] + near_y[1 : wide_x + 1] + near_y[2 : wide_x + 2]
        number = near.reshape(CH, 128) - 1.0
        at = pl.ds(pl.multiple_of(k * CH, CH), CH)
        sh = sh_ref[at, :]
        sh_b = sh.astype(BF)
        sh_l = (sh - sh_b.astype(F32)).astype(BF)
        mw = mw_ref[...]
        summed = se_ref[at, :] + mm(sh_b, mw) + mm(sh_l, mw) + number * mb_ref[...]
        inner = mm(rel_ref[at, :], nw_ref[...]) + mm(summed.astype(BF), uw_ref[...]) + nb_ref[...]
        h = inner * 0.5
        t = jnp.tanh(h)
        q = 1.0 + t
        silu = h * q
        dsilu = 0.5 * (q + silu * (1.0 - t))
        output = mm(silu.astype(BF), ow_ref[...]) + ob_ref[...]
        centred = output - jnp.mean(output, axis=-1, keepdims=True)
        inv = lax.rsqrt(jnp.mean(centred * centred, axis=-1, keepdims=True) + ln_eps)
        normed = centred * inv
        occ = occ_ref[at, :]
        gain = gain_ref[...]
        upd_ref[at, :] = (rel_ref[at, :].astype(F32) + occ * normed * gain).astype(BF)
        cot = cot_ref[at, :].astype(F32)
        gn = occ * cot * gain
        go = (
            (
                gn
                - jnp.mean(gn, axis=-1, keepdims=True)
                - normed * jnp.mean(gn * normed, axis=-1, keepdims=True)
            )
            * inv
        ).astype(BF)
        ginner = (mmt(go, ow_ref[...]) * dsilu).astype(BF)
        gsum = mmt(ginner, uw_ref[...]).astype(BF)
        pull = mmt(gsum, mw) * 0.5
        r_ref[pl.ds(k * wide_x, wide_x)] = pull.reshape(wide_x, 8, 8, 128)
        rgrad = (pull * sg_ref[at, :]).astype(BF)
        total = cot + mmt(ginner, nw_ref[...]) + mmt(rgrad, rw_ref[...])
        grad_ref[pl.ds(k * wide_x, wide_x)] = total.reshape(wide_x, 8, 8, 128)


    sf_ref[...] = jnp.zeros(sf_ref.shape, F32)

    def tiles(x, y):
        rows = (r_ref[x, y], r_ref[x + 16, y])
        return [
            jnp.concatenate(
                [jnp.broadcast_to(v[p : p + 1], (8, 128)) for v in rows], axis=0
            )
            for p in range(8)
        ]

    @pl.loop(0, 16)
    def _(x):
        for y in range(8):
            pulls = [v.astype(BF) for v in tiles(x, y)]
            for n in range(9):
                dx, dy = step_of(n)
                total = tree([g_ref[x, p, n, y * 16 : y * 16 + 16] * pulls[p] for p in range(8)])
                total = total.astype(F32)
                sf_ref[x + dx, y + dy] += total[0:8]
                sf_ref[x + 16 + dx, y + dy] += total[8:16]

    for u in range(4):
        for side in range(2):
            edge = sf_ref[1 + 8 * u : 9 + 8 * u, 9 * side].reshape(64, 128)
            by[side, u * 64 : u * 64 + 64] = edge.astype(BF)
    for side in range(2):
        x = 33 * side
        bx[side] = sf_ref[x, 1:9].reshape(64, 128).astype(BF)
        for end in range(2):
            cell = sf_ref[x, 9 * end]
            bc[2 * side + end] = jnp.concatenate([cell, jnp.zeros_like(cell)], axis=0).astype(BF)
    pairs = ((bx, dx_buf), (by, dy_buf), (bc, dc_buf))
    third = []
    for k in DIRECTIONS:
        kind, place = rim_slot(k)
        source, target = pairs[kind]
        third.append(send(k, source.at[place], target.at[place], send3, recv3))
    sw = sw_ref[...]
    for u in range(4):
        core = sf_ref[1 + 8 * u : 9 + 8 * u, 1:9].reshape(512, 128).astype(BF)
        grad_ref[8 * u : 8 * u + 8] += mmt(core, sw).reshape(8, 8, 8, 128)
    for copy in third:
        copy.wait()
    for side in range(2):
        at = 31 if side == 0 else 0
        grad_ref[at] += mmt(dx_buf[side], sw).reshape(8, 8, 128)
        at = 7 if side == 0 else 0
        grad_ref[:, at] += mmt(dy_buf[side], sw).reshape(32, 8, 128)
    corner = mmt(dc_buf[...].reshape(64, 128), sw).reshape(4, 16, 128)[:, 0:8]
    grad_ref[31, 7] += corner[0]
    grad_ref[31, 0] += corner[1]
    grad_ref[0, 7] += corner[2]
    grad_ref[0, 0] += corner[3]


def step_call(*operands):
    full = pl.BlockSpec(memory_space=pltpu.VMEM)
    rim = [(2, 64, 128), (2, 256, 128), (4, 16, 128)]
    return pl.pallas_call(
        step_kernel,
        out_shape=(
            jax.ShapeDtypeStruct((2048, 128), BF),
            jax.ShapeDtypeStruct((32, 8, 8, 128), F32),
        ),
        in_specs=[full] * len(operands),
        out_specs=(full,) * 2,
        scratch_shapes=[pltpu.VMEM((9, 96, 128), BF), pltpu.VMEM((9, 96, 128), BF)]
        + [pltpu.VMEM(v, BF) for v in rim * 4]
        + [
            pltpu.VMEM((2304, 640), BF),
            pltpu.VMEM((640, 256), BF),
            pltpu.VMEM((2048, 128), BF),
            pltpu.VMEM((34, 10, 8, 128), F32),
            pltpu.VMEM((32, 8, 8, 128), F32),
            pltpu.VMEM((34, 10, 8, 128), F32),
            pltpu.VMEM((NH, 10, 16, 128), BF),
            pltpu.VMEM((32, 8, 8, 128), F32),
            pltpu.VMEM((2048, 128), F32),
            pltpu.VMEM((34, 10, 8, 128), F32),
            pltpu.VMEM((128, 1024), BF),
            pltpu.VMEM((256, 256), BF),
            pltpu.VMEM((128, 1024), BF),
            pltpu.VMEM((2048, 128), F32),
            pltpu.VMEM((2048, 128), F32),
            pltpu.VMEM((2048, 128), F32),
            pltpu.VMEM((16, 8, 9, 128, 128), BF),
        ]
        + [pltpu.SemaphoreType.DMA((9,))] * 6,
        compiler_params=pltpu.CompilerParams(
            collective_id=0, has_side_effects=True, vmem_limit_bytes=62 * 1024 * 1024
        ),
        name="step",
    )(*operands)


def on_device(
    latent, position, counts, leaving, landing, cotangent, encoder_weight, encoder_bias,
    receiver_weight, sender_weight, edge_weight, edge_bias, message_weight, message_bias,
    node_weight, summed_weight, node_bias, output_weight, output_bias, norm_gain,
):
    occupied = (jnp.arange(8)[None, :] < counts.reshape(256, 1)).astype(BF)
    geo = jnp.concatenate([position.reshape(256, 24), occupied], axis=1)
    geo = jnp.pad(geo, ((0, 0), (0, 96)))
    line = lambda v: v.reshape(1, -1)
    updated, grad = step_call(
        latent.reshape(2048, 128), leaving.reshape(9, 64), landing.reshape(9, 64), geo,
        cotangent.reshape(2048, 128), encoder_weight, line(encoder_bias), receiver_weight,
        sender_weight, edge_weight, line(edge_bias), message_weight, line(message_bias),
        node_weight, summed_weight, line(node_bias), output_weight, line(output_bias),
        line(norm_gain),
    )
    return updated.reshape(latent.shape), grad


def solution(mesh):
    split = P("gx", "gy", None, None)
    return jax.shard_map(
        on_device,
        mesh=mesh,
        in_specs=(split, split, P("gx", "gy"), split, split, split) + (P(),) * 14,
        out_specs=(split, split),
        check_vma=False,
    )
```

time: 93.3 us -> 77.9 us (0.83)
  Pallas kernels: 82.2 us -> 70.7 us
  local copies, waits for them, and re-layouts: 10 us -> 6.25 us
    pallas_call x3 -> x1, Pallas kernels: 82.2 us -> 70.7 us  [step_call(): pl.pallas_call(step_kernel, out_shape=(jax.ShapeDtypeStruct((2048, 128),...]
    unnamed x30 -> x13, local copies, waits for them, and re-layouts: 9.55 us -> 5.15 us
where the time goes in v2:
time: 77.9 us; the launch traced here: 77.7 us
  Pallas kernels  70.7 us (91%)
  local copies, waits for them, and re-layouts  6.25 us (8%)
    pallas_call x1, Pallas kernels, step_call(): pl.pallas_call(step_kernel, out_shape=(jax.ShapeDtypeStruct((2048, 128),...  70.7 us
    unnamed x13, local copies, waits for them, and re-layouts  5.15 us

profile of v2, /device:TPU:0, one launch (start us, length us, event | category | flops | bytes accessed | tf_op | source)
XLA Modules:
  0.0 77.7 jit_solution(17156316426499077146)
XLA Ops:
  0.6 0.0 copy-start.1
  0.6 0.8 copy.27
  1.4 0.0 copy-start.3
  1.4 0.1 lt.16
  1.5 0.0 copy-start.2
  1.5 0.6 copy-done.3
  2.1 0.1 copy-done.2
  2.2 0.6 copy_bitcast_fusion
  2.8 0.0 copy-done.1
  2.8 0.2 copy.26
  3.0 0.2 reshape.45
  3.2 0.1 copy.28
  3.3 0.7 pad.4.geo_ref
  4.0 70.7 %step.1 = (bf16[2048,128]{1,0:T(8,128)(2,1)}, f32[32,8,8,128]{3,2,1,0:T(8,128)}) custom-call(bf16[2048,128]{1,0:T(8,128)(2,1)} %bitcast.17, s32[9,64]{1,0:T(8,128)} %get-tuple-element.7.leave_ref, s32[9,64]{1,0:T(8,128)} %get-tuple-element.6.land_ref, bf16[256,128]{1,0:T(8,128)(2,1)} %pad.4.geo_ref, bf16[2048,128]{1,0:T(8,128)(2,1)} %bitcast.18, ...), custom_call_target="tpu_custom_call" | custom-call | tf_op jit(solution)/shard_map/step/pallas_call | solution.py:447
  74.7 0.0 copy-start
  74.7 2.0 %copy.35 = bf16[32,8,8,128]{3,2,1,0:T(8,128)(2,1)} copy(bf16[32,8,8,128]{3,2,1,0:T(8,128)(2,1)} %bitcast.19) | data formatting | bytes 1048576
  76.7 0.0 copy-done
  76.7 1.0 %copy.36 = f32[32,8,8,128]{3,2,1,0:T(8,128)} copy(f32[32,8,8,128]{3,2,1,0:T(8,128)S(1)} %copy-done) | data formatting | bytes 2097152
  (2 shorter events, 0.0 us)
Async XLA Ops:
  0.6 2.2 %copy-start.1 = (bf16[32,8,3,8]{0,3,2,1:T(8,128)(2,1)S(1)}, bf16[32,8,3,8]{0,3,2,1:T(8,128)(2,1)}, u32[]{:S(2)}) copy-start(bf16[32,8,3,8]{0,3,2,1:T(8,128)(2,1)} %param.21) | copy-start | bytes 36868
  1.4 0.7 copy-start.3
  1.5 0.7 copy-start.2
  74.7 2.0 %copy-start = (f32[32,8,8,128]{3,2,1,0:T(8,128)S(1)}, f32[32,8,8,128]{3,2,1,0:T(8,128)}, u32[]{:S(2)}) copy-start(f32[32,8,8,128]{3,2,1,0:T(8,128)} %get-tuple-element.11) | copy-start | bytes 3145732

commit v3 on v2

--- a/solution.py
+++ b/solution.py
@@ -69,12 +69,12 @@
 
 
 def step_kernel(
-    lat_ref, leave_ref, land_ref, geo_ref, cot_ref,
+    lat_ref, leave_ref, land_ref, place_ref, count_ref, cot_ref,
     ew_ref, eb_ref, rw_ref, sw_ref, dw_ref, db_ref, mw_ref, mb_ref,
     nw_ref, uw_ref, nb_ref, ow_ref, ob_ref, gain_ref,
     upd_ref, grad_ref,
     out_buf, in_buf, sx, sy, sc, tx, ty, tc, bx, by, bc, dx_buf, dy_buf, dc_buf,
-    hot_ref, cat_ref, rel_ref,
+    hot_ref, cat_ref, rel_ref, geo_ref,
     gj_ref, gi_ref, sf_ref, s_ref, r_ref, occ_ref, cc_ref, w1_ref, bd_ref, red_ref,
     se_ref, sh_ref, sg_ref, g_ref,
     send1, recv1, send2, recv2, send3, recv3,
@@ -82,7 +82,19 @@
     barrier = pltpu.get_barrier_semaphore()
     for k in DIRECTIONS:
         pl.semaphore_signal(barrier, inc=1, device_id=neighbour(k), device_id_type=MESH)
-    leave = leave_ref[...]
+    unit = jnp.where(iota((32, 32), 0) == iota((32, 32), 1), 1.0, 0.0).astype(BF)
+    count = count_ref[...].astype(F32)
+    turned = []
+    for y in range(8):
+        held = jnp.where(iota((8, 32), 0).astype(F32) < count[y : y + 1], 1.0, 0.0)
+        lanes_x = jnp.concatenate([place_ref[y].astype(F32), held], axis=0).astype(BF)
+        turned.append(mmt(unit, lanes_x))
+    turned = jnp.concatenate(turned, axis=0).astype(BF)
+    cell_row = iota((256, 256), 0)
+    order = jnp.where(iota((256, 256), 1) == cell_row % 8 * 32 + cell_row // 8, 1.0, 0.0).astype(BF)
+    widen = jnp.where(iota((32, 128), 0) == iota((32, 128), 1), 1.0, 0.0).astype(BF)
+    geo_ref[...] = mm(mm(order, turned).astype(BF), widen).astype(BF)
+    leave = jnp.concatenate([leave_ref[0, k] for k in range(9)], axis=0)
     upper = jnp.where(leave < 0, -64, leave // 64 * 64)
     lower = (leave - upper).astype(F32)
     upper = upper.astype(F32)
@@ -118,12 +130,12 @@
             out_buf[k, 64:96] = geo_ref[first : first + 32]
     pl.semaphore_wait(barrier, 8)
     first = [send(k, out_buf.at[k], in_buf.at[k], send1, recv1) for k in DIRECTIONS]
-    land = land_ref[...]
+    land = [land_ref[0, k] for k in range(9)]
     for t in range(5):
         if t < 4:
-            row = jnp.concatenate([land[2 * t : 2 * t + 1], land[2 * t + 1 : 2 * t + 2]], axis=1)
+            row = jnp.concatenate([land[2 * t], land[2 * t + 1]], axis=1)
         else:
-            row = jnp.concatenate([land[8:9], jnp.full((1, 64), -1, jnp.int32)], axis=1)
+            row = jnp.concatenate([land[8], jnp.full((1, 64), -1, jnp.int32)], axis=1)
         for u in range(8):
             hot_ref[u * 256 : u * 256 + 256, t * 128 : t * 128 + 128] = jnp.where(
                 iota((256, 128), 0) + u * 256 == row, 1.0, 0.0
@@ -332,8 +344,10 @@
                         piece.append(stack[0][1])
                 for part, piece in zip(parts, pieces):
                     part.append(jnp.concatenate(piece, axis=0))
-        for part, out in zip(parts, (se_ref, sh_ref, sg_ref)):
-            total = mm(red_ref[...], jnp.concatenate(part, axis=0))
+        beside = [jnp.concatenate(part, axis=0) for part in parts]
+        totals = mm(red_ref[...], jnp.concatenate(beside, axis=1))
+        for c, out in enumerate((se_ref, sh_ref, sg_ref)):
+            total = totals[:, c * 128 : c * 128 + 128]
             at = pl.multiple_of(x * 64, 64)
             out[pl.ds(at, 64), :] = total[:64]
             out[pl.ds(at + 1024, 64), :] = total[64:]
@@ -458,6 +472,7 @@
             pltpu.VMEM((2304, 640), BF),
             pltpu.VMEM((640, 256), BF),
             pltpu.VMEM((2048, 128), BF),
+            pltpu.VMEM((256, 128), BF),
             pltpu.VMEM((34, 10, 8, 128), F32),
             pltpu.VMEM((32, 8, 8, 128), F32),
             pltpu.VMEM((34, 10, 8, 128), F32),
@@ -481,22 +496,59 @@
     )(*operands)
 
 
+def write_kernel(upd_ref, grad_ref, upd_out, grad_out, upd_held, grad_held, sems_in, sems_out):
+    pieces = [(grad_ref, grad_held, grad_out, pl.ds(8 * u, 8)) for u in range(4)]
+    pieces += [(upd_ref, upd_held, upd_out, pl.ds(1024 * u, 1024)) for u in range(2)]
+    entering = []
+    for place, (source, held, _, at) in enumerate(pieces):
+        entering.append(pltpu.make_async_copy(source.at[at], held.at[at], sems_in.at[place]))
+        entering[-1].start()
+    leaving = []
+    for place, (_, held, target, at) in enumerate(pieces):
+        entering[place].wait()
+        leaving.append(pltpu.make_async_copy(held.at[at], target.at[at], sems_out.at[place]))
+        leaving[-1].start()
+    for copy in leaving:
+        copy.wait()
+
+
+def write_call(updated, grad):
+    place = pl.BlockSpec(memory_space=pl.ANY)
+    return pl.pallas_call(
+        write_kernel,
+        out_shape=(
+            jax.ShapeDtypeStruct(updated.shape, BF),
+            jax.ShapeDtypeStruct(grad.shape, F32),
+        ),
+        in_specs=[place] * 2,
+        out_specs=(place,) * 2,
+        scratch_shapes=[
+            pltpu.VMEM(updated.shape, BF),
+            pltpu.VMEM(grad.shape, F32),
+            pltpu.SemaphoreType.DMA((6,)),
+            pltpu.SemaphoreType.DMA((6,)),
+        ],
+        compiler_params=pltpu.CompilerParams(vmem_limit_bytes=60 * 1024 * 1024),
+        name="write",
+    )(updated, grad)
+
+
 def on_device(
     latent, position, counts, leaving, landing, cotangent, encoder_weight, encoder_bias,
     receiver_weight, sender_weight, edge_weight, edge_bias, message_weight, message_bias,
     node_weight, summed_weight, node_bias, output_weight, output_bias, norm_gain,
 ):
-    occupied = (jnp.arange(8)[None, :] < counts.reshape(256, 1)).astype(BF)
-    geo = jnp.concatenate([position.reshape(256, 24), occupied], axis=1)
-    geo = jnp.pad(geo, ((0, 0), (0, 96)))
+    places = jnp.transpose(position, (1, 2, 3, 0)).reshape(8, 24, 32)
     line = lambda v: v.reshape(1, -1)
     updated, grad = step_call(
-        latent.reshape(2048, 128), leaving.reshape(9, 64), landing.reshape(9, 64), geo,
+        latent.reshape(2048, 128), jnp.transpose(leaving, (0, 2, 1, 3)),
+        jnp.transpose(landing, (0, 2, 1, 3)), places, jnp.transpose(counts),
         cotangent.reshape(2048, 128), encoder_weight, line(encoder_bias), receiver_weight,
         sender_weight, edge_weight, line(edge_bias), message_weight, line(message_bias),
         node_weight, summed_weight, line(node_bias), output_weight, line(output_bias),
         line(norm_gain),
     )
+    updated, grad = write_call(updated, grad)
     return updated.reshape(latent.shape), grad
 
 

time: 77.9 us -> 73.5 us (0.944)
  local copies, waits for them, and re-layouts: 6.25 us -> 0 us
  Pallas kernels: 70.7 us -> 72.7 us
    unnamed x13 -> x0, local copies, waits for them, and re-layouts: 5.15 us -> none
    pallas_call x0 -> x1, Pallas kernels: none -> 2.19 us  [write_call(): pl.pallas_call(write_kernel, out_shape=(jax.ShapeDtypeStruct(updated.shap...]
where the time goes in v3:
time: 73.5 us; the launch traced here: 73.3 us
  Pallas kernels  72.7 us (99%)
    pallas_call x1, Pallas kernels, step_call(): pl.pallas_call(step_kernel, out_shape=(jax.ShapeDtypeStruct((2048, 128),...  70.5 us
    pallas_call x1, Pallas kernels, write_call(): pl.pallas_call(write_kernel, out_shape=(jax.ShapeDtypeStruct(updated.shap...  2.19 us

profile of v3, /device:TPU:0, one launch (start us, length us, event | category | flops | bytes accessed | tf_op | source)
XLA Modules:
  0.0 73.3 jit_solution(12580037268537369)
XLA Ops:
  0.6 70.5 %step.1 = (bf16[2048,128]{1,0:T(8,128)(2,1)}, f32[32,8,8,128]{3,2,1,0:T(8,128)}) custom-call(bf16[2048,128]{1,0:T(8,128)(2,1)} %bitcast.15, s32[1,9,1,64]{3,2,1,0:T(1,128)} %bitcast.18, s32[1,9,1,64]{3,2,1,0:T(1,128)} %bitcast.19, bf16[8,24,32]{2,1,0:T(8,128)(2,1)} %bitcast.17, s32[8,32]{1,0:T(8,128)} %bitcast.20, bf16[2048,128]{1,0:T(8,128)(2,1)} %bitcast.16, ...), custom_call_target="tpu_custom_call" | custom-call | tf_op jit(solution)/shard_map/step/pallas_call | solution.py:461
  71.2 2.2 %write.1 = (bf16[2048,128]{1,0:T(8,128)(2,1)}, f32[32,8,8,128]{3,2,1,0:T(8,128)}) custom-call(bf16[2048,128]{1,0:T(8,128)(2,1)} %get-tuple-element.6.upd_ref, f32[32,8,8,128]{3,2,1,0:T(8,128)} %get-tuple-element.7.grad_ref), custom_call_target="tpu_custom_call" | custom-call | tf_op jit(solution)/shard_map/write/pallas_call | solution.py:517

commit v4 on v3

--- a/solution.py
+++ b/solution.py
@@ -326,7 +326,7 @@
                         dx, dy = step_of(n)
                         at = slice(n * 128 + y * 16, n * 128 + (y + 2) * 16)
                         near = s_ref[x + dx, dy + y : dy + y + 2].reshape(32, 128)
-                        h = hh[at, cols] + (near + r[inside])
+                        h = (hh[at, cols] + near) + r[inside]
                         if n == 4:
                             own = iota((32, 128), 0) % 8 == p
                             h = h + jnp.where(own, -BIG_H, 0.0).astype(BF)
@@ -352,7 +352,7 @@
             out[pl.ds(at, 64), :] = total[:64]
             out[pl.ds(at + 1024, 64), :] = total[64:]
 
-    CH = 512
+    CH = 1024
 
     @pl.loop(0, 2048 // CH)
     def _(k):

time: 73.5 us -> 68.9 us (0.937)
  Pallas kernels: 72.7 us -> 68.1 us
    pallas_call x1, Pallas kernels: 70.5 us -> 65.9 us  [step_call(): pl.pallas_call(step_kernel, out_shape=(jax.ShapeDtypeStruct((2048, 128),...]
where the time goes in v4:
time: 68.9 us; the launch traced here: 68.8 us
  Pallas kernels  68.1 us (99%)
    pallas_call x1, Pallas kernels, step_call(): pl.pallas_call(step_kernel, out_shape=(jax.ShapeDtypeStruct((2048, 128),...  65.9 us
    pallas_call x1, Pallas kernels, write_call(): pl.pallas_call(write_kernel, out_shape=(jax.ShapeDtypeStruct(updated.shap...  2.19 us

profile of v4, /device:TPU:0, one launch (start us, length us, event | category | flops | bytes accessed | tf_op | source)
XLA Modules:
  0.0 68.8 jit_solution(10224901771983483255)
XLA Ops:
  0.6 65.9 %step.1 = (bf16[2048,128]{1,0:T(8,128)(2,1)}, f32[32,8,8,128]{3,2,1,0:T(8,128)}) custom-call(bf16[2048,128]{1,0:T(8,128)(2,1)} %bitcast.15, s32[1,9,1,64]{3,2,1,0:T(1,128)} %bitcast.18, s32[1,9,1,64]{3,2,1,0:T(1,128)} %bitcast.19, bf16[8,24,32]{2,1,0:T(8,128)(2,1)} %bitcast.17, s32[8,32]{1,0:T(8,128)} %bitcast.20, bf16[2048,128]{1,0:T(8,128)(2,1)} %bitcast.16, ...), custom_call_target="tpu_custom_call" | custom-call | tf_op jit(solution)/shard_map/step/pallas_call | solution.py:461
  66.6 2.2 %write.1 = (bf16[2048,128]{1,0:T(8,128)(2,1)}, f32[32,8,8,128]{3,2,1,0:T(8,128)}) custom-call(bf16[2048,128]{1,0:T(8,128)(2,1)} %get-tuple-element.6.upd_ref, f32[32,8,8,128]{3,2,1,0:T(8,128)} %get-tuple-element.7.grad_ref), custom_call_target="tpu_custom_call" | custom-call | tf_op jit(solution)/shard_map/write/pallas_call | solution.py:517
